TPU v7x, 32 devices: a whole 2x2x4 slice. The times are simulated.
32 devices in a mesh: seq: 8 (over y, x, core), head: 4 (over z).
Axes of the slice: x: 2, y: 2, z: 4, core: 2. Of those that a mesh axis runs over, the one named last changes fastest.
Arguments:
- prompt_lengths: int32 [4], replicated, may hold values from 1 to 768, 1024 in all
- prefill_queries: bfloat16 [1024, 128, 576], P('seq', 'head'), may hold values from -667 to 666
- prefill_latents: bfloat16 [1024, 576], P('seq'), may hold values from -6 to 6
- group_members: int32 [64], replicated, may hold values from 0 to 63, as said below
- page_order: int32 [512], replicated, may hold values from 0 to 511, as said below
- cache_pages: bfloat16 [512, 64, 576], P('seq'), may hold values from -6 to 6
- dec_lengths: int32 [64], replicated, may hold values from 1 to 512, 20480 in all
- dec_queries: bfloat16 [64, 128, 576], P('head', 'seq'), may hold values from -667 to 666
- dec_new_latent: bfloat16 [64, 576], P('head'), may hold values from -6 to 6
- value_up: bfloat16 [128, 512, 128], P('seq'), may hold values from -0.25 to 0.25
- out_weight: bfloat16 [16384, 5120], P('seq'), may hold values from -0.046875 to 0.046875
Outputs:
- prefill_out: bfloat16 [1024, 128, 512], P('seq', 'head')
- dec_out: bfloat16 [64, 5120], P('head')
Inputs may be any that keep to these rules, and one draw needn't show every extreme that they name: Group g holds the requests group_members[g * 16] to group_members[(g + 1) * 16 - 1]; every request appears once. page_order[r * 8 + j] is the row of cache_pages that holds cached positions j * 64 to (j + 1) * 64 - 1 of request r; every page appears once; the 64 pages of each index of seq hold exactly 16 pages of the requests of each group.
All inputs are finite; a program needn't handle non-finite values.
Results may differ from a plain program's by a relative error of at most 0.014.
Values may be sent and summed in bfloat16 or wider, within the bound.
A program may use at most 192 MiB of HBM per device.

v0:
```python
import jax
import jax.numpy as jnp
from jax import lax
from jax.sharding import PartitionSpec as P

LAT = 512
ROPE = 64
VHEAD = 128
PPR = 8


big_negative = -1e30
highest_precision = lax.Precision.HIGHEST


def score_scale():
    return (VHEAD + ROPE) ** (-0.5)


def document_of(positions, prompt_lengths):
    bounds = jnp.cumsum(prompt_lengths, dtype=jnp.int32)
    return jnp.sum((positions[:, None] >= bounds[None, :]).astype(jnp.int32), axis=1)


def prefill_attention(prompt_lengths, prefill_queries, prefill_latents):
    row_count = prefill_queries.shape[0]
    heads_here = prefill_queries.shape[1]
    query_positions = lax.axis_index("seq") * row_count + jnp.arange(row_count, dtype=jnp.int32)
    query_docs = document_of(query_positions, prompt_lengths)
    key_piece = lax.all_gather(prefill_latents, "seq", axis=0, tiled=True)
    running = jnp.full((row_count, heads_here), big_negative, jnp.float32)
    key_positions = jnp.arange(key_piece.shape[0], dtype=jnp.int32)
    same_doc = document_of(key_positions, prompt_lengths)[None, :] == query_docs[:, None]
    allowed = (key_positions[None, :] <= query_positions[:, None]) & same_doc
    scores = (
        jnp.einsum("thc,kc->thk", prefill_queries, key_piece, preferred_element_type=jnp.float32)
        * score_scale()
    )
    scores = jnp.where(allowed[:, None, :], scores, big_negative)
    updated = jnp.maximum(running, jnp.max(scores, axis=2))
    weights = jnp.where(allowed[:, None, :], jnp.exp(scores - updated[:, :, None]), 0.0).astype(
        jnp.bfloat16
    )
    totals = jnp.sum(weights.astype(jnp.float32), axis=2)
    summed = jnp.einsum(
        "thk,kc->thc", weights, key_piece[:, :LAT], preferred_element_type=jnp.float32
    )
    running, totals, summed = (updated, totals, summed)
    return (summed / totals[:, :, None]).astype(jnp.bfloat16)


def page_selection(group_members, page_order, group_index, group_rows, n_seq, n_head, pages_dev):
    total_pages = page_order.shape[0]
    slot_of_page = (
        jnp.zeros((total_pages,), jnp.int32)
        .at[page_order]
        .set(jnp.arange(total_pages, dtype=jnp.int32))
    )
    request_of_page = slot_of_page // PPR
    row_of_request = (
        jnp.zeros_like(group_members)
        .at[group_members]
        .set(jnp.arange(group_members.shape[0], dtype=jnp.int32))
    )
    global_row = jnp.take(row_of_request, request_of_page)
    outside = (global_row // group_rows != group_index).astype(jnp.int32).reshape(n_seq, pages_dev)
    group_pages = pages_dev // n_head
    chosen_local = jnp.argsort(outside, axis=1, stable=True)[:, :group_pages]
    chosen = chosen_local + (jnp.arange(n_seq, dtype=jnp.int32) * pages_dev)[:, None]
    chosen_row = jnp.take(global_row, chosen) % group_rows
    chosen_slot = jnp.take(slot_of_page, chosen) % PPR
    return (chosen_local, chosen_row, chosen_slot)


def page_scores(query_rows, cached, page_rows, page_slots, limits):
    page_queries = jnp.take(query_rows, page_rows, axis=0)
    scores = (
        jnp.einsum("phc,ptc->pht", page_queries, cached, preferred_element_type=jnp.float32)
        * score_scale()
    )
    offsets = jnp.arange(cached.shape[1], dtype=jnp.int32)
    usable = (
        page_slots[:, None] * cached.shape[1] + offsets[None, :]
        < jnp.take(limits, page_rows)[:, None]
    )
    return (jnp.where(usable[:, None, :], scores, big_negative), usable)


def row_maxima(scores, page_rows, group_rows):
    member = page_rows[None, :] == jnp.arange(group_rows, dtype=jnp.int32)[:, None]
    page_max = jnp.max(scores, axis=2)
    return (
        jnp.max(jnp.where(member[:, :, None], page_max[None, :, :], big_negative), axis=1),
        member,
    )


def page_sums(scores, usable, cached, page_rows, member, highest):
    shifted = scores - jnp.take(highest, page_rows, axis=0)[:, :, None]
    weights = jnp.where(usable[:, None, :], jnp.exp(shifted), 0.0).astype(jnp.bfloat16)
    summed = jnp.einsum(
        "pht,ptc->phc", weights, cached[:, :, :LAT], preferred_element_type=jnp.float32
    )
    totals = jnp.sum(weights.astype(jnp.float32), axis=2)
    selector = member.astype(jnp.float32)
    row_summed = jnp.einsum("rp,phc->rhc", selector, summed, precision=highest_precision)
    row_totals = jnp.dot(selector, totals, precision=highest_precision)
    return (row_summed, row_totals)


def finish_rows(summed, totals, own_weight, own_latent):
    own_values = own_latent[:, None, :LAT].astype(jnp.float32)
    mixed_latent = (summed + own_weight[:, :, None] * own_values) / (totals + own_weight)[
        :, :, None
    ]
    return mixed_latent.astype(jnp.bfloat16)


def on_device(
    prompt_lengths,
    prefill_queries,
    prefill_latents,
    group_members,
    page_order,
    cache_pages,
    dec_lengths,
    dec_queries,
    dec_new_latent,
    value_up,
    out_weight,
):
    prefill_out = prefill_attention(prompt_lengths, prefill_queries, prefill_latents)
    n_seq = lax.axis_size("seq")
    n_head = lax.axis_size("head")
    holder = lax.axis_index("seq")
    group_index = lax.axis_index("head")
    requests, own_latents = (
        lax.all_gather(dec_queries, "head", axis=0, tiled=True),
        lax.all_gather(dec_new_latent, "head", axis=0, tiled=True),
    )
    group_rows = requests.shape[0] // n_head
    members = lax.dynamic_slice_in_dim(group_members, group_index * group_rows, group_rows)
    own_latent = jnp.take(own_latents, members, axis=0)
    limits = jnp.take(dec_lengths, members)
    query_rows = jnp.take(requests, members, axis=0)
    heads_here = query_rows.shape[1]
    pages_dev = cache_pages.shape[0]
    chosen_local, chosen_row, chosen_slot = page_selection(
        group_members, page_order, group_index, group_rows, n_seq, n_head, pages_dev
    )
    my_pages = jnp.take(cache_pages, jnp.take(chosen_local, holder, axis=0), axis=0)
    gathered = lax.all_gather(my_pages, "seq", axis=0, tiled=True)
    page_rows = chosen_row.reshape(-1)
    page_slots = chosen_slot.reshape(-1)
    scores, usable = page_scores(query_rows, gathered, page_rows, page_slots, limits)
    cached_max, member = row_maxima(scores, page_rows, group_rows)
    own_scores = (
        jnp.einsum("rhc,rc->rh", query_rows, own_latent, preferred_element_type=jnp.float32)
        * score_scale()
    )
    highest = jnp.maximum(cached_max, own_scores)
    summed, totals = page_sums(scores, usable, gathered, page_rows, member, highest)
    own_weight = jnp.exp(own_scores - highest).astype(jnp.bfloat16).astype(jnp.float32)
    mixed_latent = finish_rows(summed, totals, own_weight, own_latent)
    head_values = jnp.einsum(
        "rhc,hcv->rhv", mixed_latent, value_up, preferred_element_type=jnp.float32
    ).astype(jnp.bfloat16)
    head_values = head_values.reshape(group_rows, heads_here * value_up.shape[2])
    partial_value = jnp.dot(head_values, out_weight, preferred_element_type=jnp.float32)
    dec_out = lax.psum(partial_value.astype(jnp.bfloat16), "seq")
    return (prefill_out, dec_out)


def solution(mesh):
    return jax.shard_map(
        on_device,
        mesh=mesh,
        in_specs=(
            P(),
            P("seq", "head", None),
            P("seq", None),
            P(),
            P(),
            P("seq", None, None),
            P(),
            P("head", "seq", None),
            P("head", None),
            P("seq", None, None),
            P("seq", None),
        ),
        out_specs=(P("seq", "head", None), P("head", None)),
        check_vma=False,
    )
```

profile of v0, /device:TPU:0, one launch (start us, length us, event | category | flops | bytes accessed | tf_op | source)
XLA Modules:
  0.0 223.7 jit_solution(9135647536826500544)
XLA Ops:
  9.4 2.4 %scatter_custom_fusion = s32[512]{0:T(512)S(1)} fusion(s32[512]{0:T(512)S(1)} %compare_select_fusion.2, s32[512]{0:T(512)S(1)} %iota.50, s32[]{:T(128)} %constant.186.clone.1), kind=kCustom, calls=%fused_computation.119 | custom fusion | bytes 2052 | tf_op jit(solution)/shard_map/scatter | solution.py:57
  12.5 0.8 scatter_custom_fusion.1
  16.1 39.9 %select_select_fusion = s32[512]{0:T(512)S(1)} fusion(s32[512]{0:T(512)S(1)} %scatter_custom_fusion, s32[]{:T(128)} %bitcast.4, s32[]{:T(128)} %bitcast.5, s32[]{:T(128)} %bitcast.6, s32[]{:T(128)} %bitcast.7, s32[]{:T(128)} %bitcast.8, s32[]{:T(128)} %bitcast.9, s32[]{:T(128)} %bitcast.10, s32[]{:T(128)} %bitcast.11, s32[]{:T(128)} %bitcast.12, ...), kind=kLoop, calls=%fused_computation.97 | loop fusion | flops 75776 | bytes 4352 | tf_op jit(solution)/shard_map/jit(_take)/select_n | solution.py:65
  56.3 1.0 sort.17
  57.5 3.3 %gather_fusion.3 = bf16[16,64,576]{2,1,0:T(8,128)(2,1)S(1)} fusion(bf16[64,64,576]{2,1,0:T(8,128)(2,1)} %param.18, s32[1024]{0:T(1024)S(1)} %pad_clamp_fusion), kind=kCustom, calls=%fused_computation.5 | custom fusion | bytes 2359360 | tf_op jit(solution)/shard_map/jit(_take)/gather | solution.py:151
  60.8 1.3 broadcast_select_fusion
  62.2 1.3 gather_fusion.7
  63.5 1.3 gather_fusion.6
  66.2 15.0 %all_gather.15 = bf16[64,576]{1,0:T(8,128)(2,1)S(1)} all-gather(bf16[16,576]{1,0:T(8,128)(2,1)S(1)} %copy-done.4), channel_id=1, replica_groups=mesh['seq'=8,'head'=4] {'head'}, dimensions={0}, use_global_device_ids=true | all-gather | bytes 92160 | tf_op jit(solution)/shard_map/all_gather | solution.py:139
  82.7 10.0 %fusion.47 = s32[128]{0:T(128)S(1)} fusion(s32[]{:T(128)} %bitcast.70, s32[]{:T(128)} %bitcast.71, s32[]{:T(128)} %bitcast.72, s32[]{:T(128)} %bitcast.73, s32[]{:T(128)} %bitcast.74, s32[]{:T(128)} %bitcast.75, s32[]{:T(128)} %bitcast.76, s32[]{:T(128)} %bitcast.77, s32[]{:T(128)} %bitcast.78, s32[]{:T(128)} %bitcast.79, s32[]{:T(128)} %bitcast.80, ...), kind=kLoop, calls=%fused_computation.122 | loop fusion | flops 5120 | bytes 1600 | tf_op jit(solution)/shard_map/jit(_take)/select_n | solution.py:84
  93.3 1.9 gather_fusion.1
  95.3 2.4 %gather_fusion.2 = bf16[128,16,576]{2,1,0:T(8,128)(2,1)} fusion(bf16[16,16,576]{2,1,0:T(8,128)(2,1)S(1)} %broadcast_select_fusion.1, s32[1024]{0:T(1024)S(1)} %pad_clamp_fusion.1), kind=kCustom, calls=%fused_computation.4 | custom fusion | bytes 4719104 | tf_op jit(solution)/shard_map/jit(_take)/gather | solution.py:76
  97.9 10.4 %fusion = (f32[128,32]{0,1:T(8,128)S(1)}, f32[128,32,1024]{2,0,1:T(8,128)S(1)}) fusion(pred[128,1024]{1,0:T(8,128)(4,1)S(1)} %fusion.27, bf16[128,32,576]{0,2,1:T(8,128)(2,1)} %param.14, bf16[1024,576]{0,1:T(8,128)(2,1)} %all-gather.4.cloned.1.call-done), kind=kOutput, calls=%fused_computation.13 | convolution fusion | flops 4844417024 | bytes 22822912 | tf_op jit(solution)/shard_map/thc,kc->thk/dot_general | solution.py:36
  108.3 5.7 %copy-done.3 = f32[128,32,1024]{2,0,1:T(8,128)} copy-done((f32[128,32,1024]{2,0,1:T(8,128)}, f32[128,32,1024]{2,0,1:T(8,128)S(1)}, u32[]{:S(2)}) %copy-start.3) | copy-done | bytes 16777240
  114.1 5.3 %convert_reduce_fusion = f32[128,32]{0,1:T(8,128)S(1)} fusion(f32[128,32]{0,1:T(8,128)S(1)} %broadcast_maximum_fusion, f32[128,32,1024]{2,0,1:T(8,128)S(1)} %get-tuple-element.119, pred[128,1024]{1,0:T(8,128)(4,1)S(1)} %fusion.27), kind=kLoop, calls=%fused_computation.10 | loop fusion | flops 29356032 | bytes 16941056 | tf_op jit(solution)/shard_map/reduce_sum | solution.py:44
  119.4 16.0 %all-gather.8.cloned.1.call-done = bf16[128,64,576]{2,1,0:T(8,128)(2,1)} async-done(((bf16[16,64,576]{2,1,0:T(8,128)(2,1)}), bf16[128,64,576]{2,1,0:T(8,128)(2,1)}) %all-gather.8.cloned.1.call-update) | async-done | bytes 9437200 | tf_op jit(solution)/shard_map/all_gather | solution.py:152
  135.4 8.3 %fusion.59 = (f32[128,16]{1,0:T(8,128)S(1)}, f32[128,16,64]{2,1,0:T(8,128)S(1)}) fusion(bf16[128,64,576]{2,1,0:T(8,128)(2,1)} %all-gather.8.cloned.1.call-done, bf16[128,16,576]{2,1,0:T(8,128)(2,1)} %gather_fusion.2, pred[128]{0:T(512)(128)(4,1)S(1)} %compare_and_fusion.3, pred[128,64]{1,0:T(8,128)(4,1)S(1)} %add_compare_fusion), kind=kOutput, calls=%fused_computation.137 | convolution fusion | flops 152565760 | bytes 12337280 | tf_op jit(solution)/shard_map/phc,ptc->pht/dot_general | solution.py:78
  145.6 4.5 %fusion.1 = f32[128,16,512]{2,1,0:T(8,128)S(1)} fusion(bf16[128,64,576]{2,1,0:T(8,128)(2,1)} %all-gather.8.cloned.1.call-done, f32[128,16,64]{2,1,0:T(8,128)S(1)} %get-tuple-element.121, f32[128,16]{1,0:T(8,128)S(1)} %broadcast_select_fusion.2, pred[128,64]{1,0:T(8,128)(4,1)S(1)} %add_compare_fusion), kind=kOutput, calls=%fused_computation.14 | convolution fusion | flops 134610944 | bytes 13123584 | tf_op jit(solution)/shard_map/pht,ptc->phc/dot_general | solution.py:101
  150.1 3.9 %fusion.21 = bf16[16,16,512]{2,0,1:T(8,128)(2,1)S(1)} fusion(f32[128,16,512]{2,1,0:T(8,128)S(1)} %fusion.1, f32[16,16]{0,1:T(8,128)S(1)} %copy.107, f32[16,512]{1,0:T(8,128)S(1)} %slice_convert_fusion, f32[16,16]{0,1:T(8,128)S(1)} %copy.106, s32[128]{0:T(128)S(1)} %eq.42), kind=kOutput, calls=%fused_computation.29 | convolution fusion | flops 201852928 | bytes 4491776 | tf_op jit(solution)/shard_map/rp,phc->rhc/dot_general | solution.py:106
  154.3 9.1 %convolution_convert_fusion = bf16[16,5120]{1,0:T(8,128)(2,1)} fusion(bf16[2048,5120]{1,0:T(8,128)(2,1)} %param.23, bf16[16,2,8,128]{3,2,1,0:T(8,128)(2,1)S(1)} %fusion.26), kind=kOutput, calls=%fused_computation.17 | convolution fusion | flops 335626240 | bytes 21200896 | tf_op jit(solution)/shard_map/dot_general | solution.py:169
  163.5 10.0 %divide_convert_fusion = bf16[128,32,512]{2,0,1:T(8,128)(2,1)S(1)} fusion(f32[128,32]{0,1:T(8,128)S(1)} %convert_reduce_fusion, bf16[1024,576]{0,1:T(8,128)(2,1)} %all-gather.4.cloned.1.call-done, f32[128,32,1024]{2,0,1:T(8,128)} %copy-done.3, f32[128,32]{0,1:T(8,128)S(1)} %broadcast_maximum_fusion, pred[128,1024]{1,0:T(8,128)(4,1)S(1)} %fusion.27), kind=kOutput, calls=%fused_computation.16 | convolution fusion | flops 4320133120 | bytes 22183936 | tf_op jit(solution)/shard_map/thk,kc->thc/dot_general | solution.py:45
  173.5 4.4 %copy.109 = bf16[128,32,512]{2,1,0:T(8,128)(2,1)} copy(bf16[128,32,512]{2,0,1:T(8,128)(2,1)S(1)} %divide_convert_fusion) | data formatting | bytes 8388608
  177.9 37.7 %all-reduce.2.cloned.1.call-done = bf16[16,5120]{1,0:T(8,128)(2,1)} async-done(((bf16[16,5120]{1,0:T(8,128)(2,1)}), bf16[16,5120]{1,0:T(8,128)(2,1)}) %all-reduce.2.cloned.1.call-update) | async-done | bytes 163856 | tf_op jit(solution)/shard_map/psum | solution.py:170
  215.6 1.6 copy.130
  (82 shorter events, 12.2 us)
Async XLA Ops:
  7.2 146.8 %copy-start = (bf16[16,512,128]{2,1,0:T(8,128)(2,1)S(1)}, bf16[16,512,128]{2,1,0:T(8,128)(2,1)}, u32[]{:S(2)}) copy-start(bf16[16,512,128]{2,1,0:T(8,128)(2,1)} %param.22) | copy-start | bytes 6291460
  7.2 86.1 %all-gather.6.cloned.1.call-start = ((), (), s32[]{:S(2)}) async-start(), calls=%async_computation.1 | async-start | bytes 1638400 | tf_op jit(solution)/shard_map/all_gather | solution.py:138
  7.9 90.0 %all-gather.4.cloned.1.call-start = ((), (), s32[]{:S(2)}) async-start(), calls=%async_computation | async-start | bytes 1327104 | tf_op jit(solution)/shard_map/all_gather | solution.py:30
  8.7 126.7 %all-gather.8.cloned.1.call-start = ((), (), s32[]{:S(2)}) async-start(), calls=%async_computation.2 | async-start | bytes 11796480 | tf_op jit(solution)/shard_map/all_gather | solution.py:152
  62.0 3.1 %copy-start.6 = (s32[4]{0:T(128)S(1)}, s32[4]{0:T(128)}, u32[]{:S(2)}) copy-start(s32[4]{0:T(128)} %param.13) | copy-start | bytes 52
  62.1 3.3 %copy-start.5 = (s32[64]{0:T(128)S(1)}, s32[64]{0:T(128)}, u32[]{:S(2)}) copy-start(s32[64]{0:T(128)} %param.16) | copy-start | bytes 772
  62.1 3.4 %copy-start.2 = (s32[64]{0:T(128)S(1)}, s32[64]{0:T(128)}, u32[]{:S(2)}) copy-start(s32[64]{0:T(128)} %param.19) | copy-start | bytes 772
  62.1 4.1 %copy-start.4 = (bf16[16,576]{1,0:T(8,128)(2,1)S(1)}, bf16[16,576]{1,0:T(8,128)(2,1)}, u32[]{:S(2)}) copy-start(bf16[16,576]{1,0:T(8,128)(2,1)} %param.21) | copy-start | bytes 55300
  62.1 153.5 %all-reduce.2.cloned.1.call-start = ((), (), s32[]{:S(2)}) async-start(), calls=%async_computation.3 | async-start | bytes 327680 | tf_op jit(solution)/shard_map/psum | solution.py:170
  108.3 5.8 %copy-start.3 = (f32[128,32,1024]{2,0,1:T(8,128)}, f32[128,32,1024]{2,0,1:T(8,128)S(1)}, u32[]{:S(2)}) copy-start(f32[128,32,1024]{2,0,1:T(8,128)S(1)} %get-tuple-element.119) | copy-start | bytes 50331652
  163.5 53.7 %copy-start.1 = (bf16[16,512,128]{2,1,0:T(8,128)(2,1)S(1)}, bf16[16,512,128]{2,1,0:T(8,128)(2,1)}, u32[]{:S(2)}) copy-start(bf16[16,512,128]{2,1,0:T(8,128)(2,1)} %param.22) | copy-start | bytes 6291460
Sparse Core Ops, SparseCore 0:
  9.6 35.4 all-gather.5
  46.9 23.1 all-gather.3
  72.0 63.3 all-gather.7
  163.6 51.9 all-reduce.1
where the time goes:
time: 225 us; the launch traced here: 224 us
  other arithmetic  61 us (27%)
  waiting for transfers between devices  55.1 us (24%)
  matrix products  46.9 us (21%)
  local copies, waits for them, and re-layouts  31.4 us (14%)
  blocking collectives  15 us (7%)
  between operations  14.1 us (6%)
    select_n x1, other arithmetic, page_selection(): global_row = jnp.take(row_of_request, request_of_page)  39.9 us
    psum x1, waiting for transfers between devices, on_device(): dec_out = lax.psum(partial_value.astype(jnp.bfloat16), 'seq')  37.7 us
    all_gather x1, waiting for transfers between devices, on_device(): gathered = lax.all_gather(my_pages, 'seq', axis=0, tiled=True)  16 us
    all_gather x1, blocking collectives, on_device(): lax.all_gather(dec_new_latent, 'head', axis=0, tiled=True)  15 us
    unnamed x16, local copies, waits for them, and re-layouts  11.8 us
    dot_general x1, matrix products, prefill_attention(): jnp.einsum('thc,kc->thk', prefill_queries, key_piece, preferred_element_t...  10.4 us
    select_n x2, other arithmetic, page_scores(): jnp.take(limits, page_rows)[:, None]  10 us
    dot_general x1, matrix products, prefill_attention(): jnp.einsum('thk,kc->thc', weights, key_piece[:, :LAT], preferred_element_...  10 us
  transfers between devices with their start and end apart: 4, of which 2 were waited for; matrix products, arithmetic and copies ran while one was open for 46% of the time, Pallas kernels for 0%

commit v1 on v0

v1 whole, which is shorter than its diff:
```python
import functools

import jax
import jax.numpy as jnp
from jax import lax
from jax.experimental import pallas as pl
from jax.experimental.pallas import tpu as pltpu
from jax.sharding import PartitionSpec as P

LAT = 512
ROPE = 64
VHEAD = 128
PPR = 8
STAT = 128

big_negative = -1e30
log2_e = 1.4426950408889634
score_scale = (VHEAD + ROPE) ** (-0.5) * log2_e
f32 = jnp.float32
bf16 = jnp.bfloat16


def prefill_kernel(lengths_ref, q_ref, kt_ref, out_ref, bias, keys, keys_t, queries):
    blocks, width, rows = kt_ref.shape
    total = blocks * rows
    heads = q_ref.shape[0]

    @pl.when(pl.program_id(0) == 0)
    def _():
        t = lax.broadcasted_iota(jnp.int32, (rows, total), 0) + lax.axis_index("seq") * rows
        k = lax.broadcasted_iota(jnp.int32, (rows, total), 1)
        bound = jnp.int32(0)
        start = jnp.zeros((rows, total), jnp.int32)
        for i in range(lengths_ref.shape[0]):
            bound = bound + lengths_ref[i]
            start = jnp.where(t >= bound, bound, start)
        bias[...] = jnp.where((k <= t) & (k >= start), 0.0, big_negative)
        for b in range(blocks):
            keys_t[:, b * rows : (b + 1) * rows] = kt_ref[b]
            keys[b * rows : (b + 1) * rows, :] = kt_ref[b, :LAT, :].T

    for h in range(heads):
        queries[h * rows : (h + 1) * rows, :] = q_ref[h].T
    for h in range(heads):
        scores = jnp.dot(
            queries[h * rows : (h + 1) * rows, :], keys_t[...], preferred_element_type=f32
        )
        scores = scores * score_scale + bias[...]
        top = jnp.max(scores, axis=1, keepdims=True)
        weights = jnp.exp2(scores - top).astype(bf16)
        sums = jnp.sum(weights.astype(f32), axis=1, keepdims=True)
        mixed = jnp.dot(weights, keys[...], preferred_element_type=f32)
        out_ref[h] = (mixed / sums).astype(bf16)


def prefill(prompt_lengths, queries, latents_t):
    rows, heads, width = queries.shape
    blocks = latents_t.shape[0]
    step = max(1, 512 // rows)
    total = blocks * rows
    out = pl.pallas_call(
        prefill_kernel,
        grid=(heads // step,),
        in_specs=[
            pl.BlockSpec(memory_space=pltpu.SMEM),
            pl.BlockSpec((step, width, rows), lambda i: (i, 0, 0)),
            pl.BlockSpec((blocks, width, rows), lambda i: (0, 0, 0)),
        ],
        out_specs=pl.BlockSpec((step, rows, LAT), lambda i: (i, 0, 0)),
        out_shape=jax.ShapeDtypeStruct((heads, rows, LAT), bf16),
        scratch_shapes=[
            pltpu.VMEM((rows, total), f32),
            pltpu.VMEM((total, LAT), bf16),
            pltpu.VMEM((width, total), bf16),
            pltpu.VMEM((step * rows, width), bf16),
        ],
        compiler_params=pltpu.CompilerParams(vmem_limit_bytes=40 << 20),
        cost_estimate=pl.CostEstimate(
            flops=2 * heads * rows * total * (width + LAT),
            bytes_accessed=2 * heads * rows * (width + LAT),
            transcendentals=heads * rows * total,
        ),
        name="prefill_attention",
    )(prompt_lengths, jnp.transpose(queries, (1, 2, 0)), latents_t)
    return jnp.transpose(out, (1, 0, 2))


def decode_kernel(order_ref, lengths_ref, q_ref, own_ref, cache_ref, out_ref, top, total, acc, todo):
    n_seq, rows, heads, width = q_ref.shape
    pages, page = cache_ref.shape[:2]
    all_heads = n_seq * heads
    seq = lax.axis_index("seq")
    first = lax.axis_index("head") * rows

    for r in range(rows):
        mine = r % n_seq == seq

        @pl.when(mine)
        def _():
            q = q_ref[:, r].reshape(all_heads, width).astype(f32)
            own = own_ref[r : r + 1, :].astype(f32)
            top[r] = jnp.sum(q * own, axis=1, keepdims=True) * score_scale
            total[r] = jnp.ones((all_heads, 1), f32)
            acc[r] = jnp.broadcast_to(own[:, :LAT], (all_heads, LAT))

        @pl.when(jnp.logical_not(mine))
        def _():
            top[r] = jnp.full((all_heads, 1), big_negative, f32)
            total[r] = jnp.zeros((all_heads, 1), f32)
            acc[r] = jnp.zeros((all_heads, LAT), f32)

    def collect(i, count):
        r = i // PPR
        place = order_ref[first * PPR + i]
        limit = lengths_ref[first + r] - (i % PPR) * page
        use = (place // pages == seq) & (limit > 0)
        todo[0, count] = r
        todo[1, count] = place % pages
        todo[2, count] = limit
        return count + use.astype(jnp.int32)

    count = lax.fori_loop(0, rows * PPR, collect, jnp.int32(0))

    def one(i, carry):
        r = todo[0, i]
        keys = cache_ref[todo[1, i]]
        q = q_ref[:, r].reshape(all_heads, width)
        scores = (
            lax.dot_general(q, keys, (((1,), (1,)), ((), ())), preferred_element_type=f32)
            * score_scale
        )
        spot = lax.broadcasted_iota(jnp.int32, scores.shape, 1)
        scores = jnp.where(spot < todo[2, i], scores, big_negative)
        before = top[r]
        now = jnp.maximum(before, jnp.max(scores, axis=1, keepdims=True))
        keep = jnp.exp2(before - now)
        weights = jnp.exp2(scores - now).astype(bf16)
        top[r] = now
        total[r] = total[r] * keep + jnp.sum(weights.astype(f32), axis=1, keepdims=True)
        acc[r] = acc[r] * keep + jnp.dot(weights, keys[:, :LAT], preferred_element_type=f32)
        return carry

    lax.fori_loop(0, count, one, 0)

    lane = lax.broadcasted_iota(jnp.int32, (all_heads, STAT), 1)

    def finish(r, carry):
        sums = total[r]
        some = sums > 0
        sums = jnp.where(some, sums, 1.0)
        mixed = (acc[r] / sums).astype(bf16)
        level = jnp.where(some, top[r] + jnp.log2(sums), big_negative)
        high = level.astype(bf16).astype(f32)
        middle = (level - high).astype(bf16).astype(f32)
        low = level - high - middle
        stat = jnp.where(lane == 0, high, jnp.where(lane == 1, middle, low)).astype(bf16)
        out_ref[:, r, :, :LAT] = mixed.reshape(n_seq, heads, LAT)
        out_ref[:, r, :, LAT:] = stat.reshape(n_seq, heads, STAT)
        return carry

    lax.fori_loop(0, rows, finish, 0)


def decode(page_order, dec_lengths, queries, own_latents, cache_pages):
    n_seq, rows, heads, width = queries.shape
    vmem = pl.BlockSpec(memory_space=pltpu.VMEM)
    smem = pl.BlockSpec(memory_space=pltpu.SMEM)
    return pl.pallas_call(
        decode_kernel,
        in_specs=[smem, smem, vmem, vmem, vmem],
        out_specs=vmem,
        out_shape=jax.ShapeDtypeStruct((n_seq, rows, heads, LAT + STAT), bf16),
        scratch_shapes=[
            pltpu.VMEM((rows, n_seq * heads, 1), f32),
            pltpu.VMEM((rows, n_seq * heads, 1), f32),
            pltpu.VMEM((rows, n_seq * heads, LAT), f32),
            pltpu.SMEM((3, rows * PPR + 1), jnp.int32),
        ],
        compiler_params=pltpu.CompilerParams(vmem_limit_bytes=48 << 20),
        name="decode_attention",
    )(page_order, dec_lengths, queries, own_latents, cache_pages)


def tail_kernel(
    n_seq, n_head, part_ref, select_ref, value_hbm, weight_hbm, out_ref,
    got, mixed, values, value, weight, sums_out, sums_in, final, zrows, chosen, gathered,
    local_sem, send_a, recv_a, send_b, recv_b, send_c, recv_c, send_d, recv_d,
):
    rows = part_ref.shape[1]
    heads = part_ref.shape[2]
    owners, _, chunk = weight.shape
    seq = lax.axis_index("seq")
    head = lax.axis_index("head")

    def seq_peer(d):
        return lax.rem(seq + d, n_seq)

    def head_peer(d):
        return lax.rem(head + d, n_head)

    weight_copies = []
    value_copy = pltpu.make_async_copy(value_hbm, value, local_sem.at[owners])
    value_copy.start()
    for step in range(owners):
        d = (step + 1) % owners
        c = lax.rem(seq + d, owners)
        copy = pltpu.make_async_copy(
            weight_hbm.at[:, pl.ds(pl.multiple_of(c * chunk, chunk), chunk)],
            weight.at[d],
            local_sem.at[d],
        )
        copy.start()
        weight_copies.append(copy)

    barrier = pltpu.get_barrier_semaphore()
    for d in range(1, n_seq):
        pl.semaphore_signal(
            barrier, inc=1, device_id=(seq_peer(d), head), device_id_type=pl.DeviceIdType.MESH
        )
    for d in range(1, n_head):
        pl.semaphore_signal(
            barrier, inc=1, device_id=(seq, head_peer(d)), device_id_type=pl.DeviceIdType.MESH
        )
    pl.semaphore_wait(barrier, n_seq + n_head - 2)

    def to_seq(source, target, send, recv, d):
        copy = pltpu.make_async_remote_copy(
            src_ref=source,
            dst_ref=target,
            send_sem=send.at[d],
            recv_sem=recv.at[d],
            device_id=(seq_peer(d), head),
            device_id_type=pl.DeviceIdType.MESH,
        )
        copy.start()
        return copy

    first = [
        to_seq(part_ref.at[seq_peer(d)], got.at[d], send_a, recv_a, d) for d in range(1, n_seq)
    ]
    for copy in first:
        copy.wait()

    def piece(d):
        return part_ref[seq] if d == 0 else got[d]

    def level_of(x):
        return (
            x[:, :, LAT : LAT + 1].astype(f32)
            + x[:, :, LAT + 1 : LAT + 2].astype(f32)
            + x[:, :, LAT + 2 : LAT + 3].astype(f32)
        )

    levels = [level_of(piece(d)) for d in range(n_seq)]
    top = functools.reduce(jnp.maximum, levels)
    shares = [jnp.exp2(level - top) for level in levels]
    total = functools.reduce(jnp.add, shares)
    result = jnp.zeros((rows, heads, LAT), f32)
    for d in range(n_seq):
        result = result + (shares[d] / total) * piece(d)[:, :, :LAT].astype(f32)
    mixed[...] = result

    value_copy.wait()
    for h in range(heads):
        values[:, h * VHEAD : (h + 1) * VHEAD] = jnp.dot(
            mixed[:, h, :].astype(bf16), value[h], preferred_element_type=f32
        ).astype(bf16)

    second = {}
    for step in range(owners):
        slot = (step + 1) % owners
        weight_copies[step].wait()
        sums_out[slot] = jnp.dot(values[...], weight[slot], preferred_element_type=f32).astype(bf16)
        for d in range(slot, n_seq, owners):
            if d:
                second[d] = to_seq(sums_out.at[slot], sums_in.at[d], send_b, recv_b, d)
    summed = sums_out[0].astype(f32)
    for d, copy in second.items():
        copy.wait()
        summed = summed + sums_in[d].astype(f32)
    final[...] = summed.astype(bf16)
    zrows[head] = summed.astype(bf16)
    third = []
    for d in range(1, n_head):
        copy = pltpu.make_async_remote_copy(
            src_ref=final,
            dst_ref=zrows.at[head],
            send_sem=send_c.at[d],
            recv_sem=recv_c.at[d],
            device_id=(seq, head_peer(d)),
            device_id_type=pl.DeviceIdType.MESH,
        )
        copy.start()
        third.append(copy)
    for copy in third:
        copy.wait()
    picked = jnp.dot(
        select_ref[...], zrows[...].reshape(n_head * rows, chunk), preferred_element_type=f32
    ).astype(bf16)
    chosen[...] = picked
    gathered[seq] = picked
    last = [to_seq(chosen, gathered.at[seq], send_d, recv_d, d) for d in range(1, n_seq)]
    for copy in last:
        copy.wait()
    for c in range(owners):
        out_ref[:, c * chunk : (c + 1) * chunk] = gathered[c]


def tail(part, select, value_up, out_weight, n_head):
    n_seq, rows, heads, wide = part.shape
    depth, width = out_weight.shape
    owners = n_seq
    while width // owners % 128:
        owners //= 2
    chunk = width // owners
    vmem = pl.BlockSpec(memory_space=pltpu.VMEM)
    anywhere = pl.BlockSpec(memory_space=pl.ANY)
    dma = pltpu.SemaphoreType.DMA
    return pl.pallas_call(
        functools.partial(tail_kernel, n_seq, n_head),
        in_specs=[vmem, vmem, anywhere, anywhere],
        out_specs=vmem,
        out_shape=jax.ShapeDtypeStruct((rows, width), bf16),
        scratch_shapes=[
            pltpu.VMEM((n_seq, rows, heads, wide), bf16),
            pltpu.VMEM((rows, heads, LAT), f32),
            pltpu.VMEM((rows, depth), bf16),
            pltpu.VMEM(value_up.shape, bf16),
            pltpu.VMEM((owners, depth, chunk), bf16),
            pltpu.VMEM((owners, rows, chunk), bf16),
            pltpu.VMEM((n_seq, rows, chunk), bf16),
            pltpu.VMEM((rows, chunk), bf16),
            pltpu.VMEM((n_head, rows, chunk), bf16),
            pltpu.VMEM((rows, chunk), bf16),
            pltpu.VMEM((n_seq, rows, chunk), bf16),
            dma((owners + 1,)),
            dma((n_seq,)), dma((n_seq,)),
            dma((n_seq,)), dma((n_seq,)),
            dma((n_head,)), dma((n_head,)),
            dma((n_seq,)), dma((n_seq,)),
        ],
        compiler_params=pltpu.CompilerParams(
            collective_id=1, has_side_effects=True, vmem_limit_bytes=52 << 20
        ),
        name="output_projection",
    )(part, select, value_up, out_weight)


def on_device(
    prompt_lengths,
    prefill_queries,
    prefill_latents,
    group_members,
    page_order,
    cache_pages,
    dec_lengths,
    dec_queries,
    dec_new_latent,
    value_up,
    out_weight,
):
    n_head = lax.axis_size("head")
    rows = dec_queries.shape[0]
    latents_t = lax.all_gather(prefill_latents.T, "seq", axis=0)
    queries = lax.all_gather(dec_queries, "seq", axis=0)
    prefill_out = prefill(prompt_lengths, prefill_queries, latents_t)
    part = decode(page_order, dec_lengths, queries, dec_new_latent, cache_pages)
    members = lax.dynamic_slice_in_dim(group_members, lax.axis_index("head") * rows, rows)
    select = jax.nn.one_hot(members, n_head * rows, dtype=bf16)
    dec_out = tail(part, select, value_up, out_weight, n_head)
    return (prefill_out, dec_out)


def solution(mesh):
    return jax.shard_map(
        on_device,
        mesh=mesh,
        in_specs=(
            P(),
            P("seq", "head", None),
            P("seq", None),
            P(),
            P(),
            P("seq", None, None),
            P(),
            P("head", "seq", None),
            P("head", None),
            P("seq", None, None),
            P("seq", None),
        ),
        out_specs=(P("seq", "head", None), P("head", None)),
        check_vma=False,
    )
```

time: 225 us -> 145 us (0.64)
  Pallas kernels: 0 us -> 86.4 us
  other arithmetic: 61 us -> 0.07 us
  matrix products: 46.9 us -> 0 us
  waiting for transfers between devices: 55.1 us -> 30.5 us
  local copies, waits for them, and re-layouts: 31.4 us -> 13.3 us
  blocking collectives: 15 us -> 0 us
    pallas_call x0 -> x3, Pallas kernels: none -> 86.4 us  [the longest x1 52.8 us: tail(): pl.pallas_call(functools.partial(tail_kernel, n_seq, n_head), in_specs=[v...]
    select_n x14 -> x0, other arithmetic: 53 us -> none  [the longest x1 39.9 us: page_selection(): global_row = jnp.take(row_of_request, request_of_page)]
    dot_general x9 -> x0, matrix products: 46.9 us -> none  [the longest x1 10.4 us: prefill_attention(): jnp.einsum('thc,kc->thk', prefill_queries, key_piece, preferred_element_t...]
    psum x1 -> x0, waiting for transfers between devices: 37.7 us -> none  [on_device(): dec_out = lax.psum(partial_value.astype(jnp.bfloat16), 'seq')]
    gather x15 -> x0, local copies, waits for them, and re-layouts: 15.7 us -> none  [the longest x1 3.27 us: on_device(): jnp.take(cache_pages, jnp.take(chosen_local, holder, axis=0), axis=0)]
    all_gather x1 -> x0, blocking collectives: 15 us -> none  [on_device(): lax.all_gather(dec_new_latent, 'head', axis=0, tiled=True)]
    all_gather x3 -> x2, waiting for transfers between devices: 16 us -> 29.1 us  [the longest x1 27.2 us: on_device(): latents_t = lax.all_gather(prefill_latents.T, 'seq', axis=0)]
    reduce_sum x4 -> x0, other arithmetic: 6.12 us -> none  [the longest x1 5.29 us: prefill_attention(): totals = jnp.sum(weights.astype(jnp.float32), axis=2)]
  transfers between devices with their start and end apart: 4 -> 2, of which waited for: 2 -> 2; matrix products, arithmetic and copies ran while one was open for 46% -> 4% of each run, Pallas kernels for 0% -> 15%
where the time goes in v1:
time: 145 us; the launch traced here: 144 us
  Pallas kernels  86.4 us (60%)
  waiting for transfers between devices  30.5 us (21%)
  between operations  14.1 us (10%)
  local copies, waits for them, and re-layouts  13.3 us (9%)
    pallas_call x1, Pallas kernels, tail(): pl.pallas_call(functools.partial(tail_kernel, n_seq, n_head), in_specs=[v...  52.8 us
    all_gather x1, waiting for transfers between devices, on_device(): latents_t = lax.all_gather(prefill_latents.T, 'seq', axis=0)  27.2 us
    pallas_call x1, Pallas kernels, prefill(): pl.pallas_call(prefill_kernel, grid=(heads // step,), in_specs=[pl.BlockS...  21.5 us
    unnamed x18, local copies, waits for them, and re-layouts  12.6 us
    pallas_call x1, Pallas kernels, decode(): pl.pallas_call(decode_kernel, in_specs=[smem, smem, vmem, vmem, vmem], ou...  12.1 us
  transfers between devices with their start and end apart: 2, of which 2 were waited for; matrix products, arithmetic and copies ran while one was open for 4% of the time, Pallas kernels for 15%

profile of v1, /device:TPU:0, one launch (start us, length us, event | category | flops | bytes accessed | tf_op | source)
XLA Modules:
  0.0 144.5 jit_solution(3816931097208624858)
XLA Ops:
  7.2 0.0 all-gather.5.cloned.1.call-start
  7.2 0.7 all-gather.5.cloned.1.call-update
  7.9 0.0 all-gather.7.cloned.1.call-start
  7.9 0.7 all-gather.7.cloned.1.call-update
  8.7 0.7 dynamic_slice.3
  9.4 0.1 fusion.select_ref
  9.5 27.2 %all-gather.5.cloned.1.call-done = bf16[4608,128]{1,0:T(8,128)(2,1)} async-done(((bf16[576,128]{1,0:T(8,128)(2,1)}), bf16[4608,128]{1,0:T(8,128)(2,1)}) %all-gather.5.cloned.1.call-update) | async-done | bytes 1179664 | tf_op jit(solution)/shard_map/all_gather | solution.py:364
  36.7 2.3 %copy-done.5 = bf16[128,32,576]{0,2,1:T(8,128)(2,1)S(1)} copy-done((bf16[128,32,576]{0,2,1:T(8,128)(2,1)S(1)}, bf16[128,32,576]{0,2,1:T(8,128)(2,1)}, u32[]{:S(2)}) %copy-start.5) | copy-done | bytes 4718616
  39.0 1.3 copy-done.6
  40.3 0.7 copy-done.7
  40.9 21.5 %prefill_attention.1 = bf16[32,128,512]{2,1,0:T(8,128)(2,1)S(1)} custom-call(s32[4]{0:T(128)S(1)} %copy-done.7, bf16[32,576,128]{2,1,0:T(8,128)(2,1)S(1)} %bitcast.7, bf16[8,576,128]{2,1,0:T(8,128)(2,1)S(1)} %bitcast.8), custom_call_target="tpu_custom_call" | custom-call | flops 9126805504 | bytes 8912896 | tf_op jit(solution)/shard_map/prefill_attention/pallas_call | solution.py:61
  62.4 0.0 copy-start.2
  62.4 0.0 copy-start.3
  62.5 0.0 copy-start.4
  62.5 4.4 %copy.14 = bf16[128,32,512]{2,1,0:T(8,128)(2,1)} copy(bf16[128,32,512]{2,0,1:T(8,128)(2,1)S(1)} %bitcast.5) | data formatting | bytes 8388608
  66.8 1.9 %all-gather.7.cloned.1.call-done = bf16[128,16,576]{2,1,0:T(8,128)(2,1)} async-done(((bf16[16,16,576]{2,1,0:T(8,128)(2,1)}), bf16[128,16,576]{2,1,0:T(8,128)(2,1)}) %all-gather.7.cloned.1.call-update) | async-done | bytes 2359312 | tf_op jit(solution)/shard_map/all_gather | solution.py:365
  68.8 0.0 copy-done.2
  68.8 0.0 copy-done.3
  68.8 1.7 %copy-done.1 = bf16[128,16,576]{2,1,0:T(8,128)(2,1)S(1)} copy-done((bf16[128,16,576]{2,1,0:T(8,128)(2,1)S(1)}, bf16[128,16,576]{2,1,0:T(8,128)(2,1)}, u32[]{:S(2)}) %copy-start.1) | copy-done | bytes 2359320
  70.5 12.1 %decode_attention.1.part_ref = bf16[8,16,16,640]{3,2,1,0:T(8,128)(2,1)S(1)} custom-call(s32[512]{0:T(512)S(1)} %copy-done.3, s32[64]{0:T(128)S(1)} %copy-done.4, bf16[8,16,16,576]{3,2,1,0:T(8,128)(2,1)S(1)} %bitcast.6, bf16[16,576]{1,0:T(8,128)(2,1)S(1)} %copy-done.2, bf16[64,64,576]{2,1,0:T(8,128)(2,1)} %cache_ref.1), custom_call_target="tpu_custom_call" | custom-call | tf_op jit(solution)/shard_map/decode_attention/pallas_call | solution.py:168
  82.6 0.0 copy-start
  82.6 1.5 %copy-done = bf16[8,16,16,640]{3,2,1,0:T(8,128)(2,1)} copy-done((bf16[8,16,16,640]{3,2,1,0:T(8,128)(2,1)}, bf16[8,16,16,640]{3,2,1,0:T(8,128)(2,1)S(1)}, u32[]{:S(2)}) %copy-start) | copy-done | bytes 2621464
  84.1 52.8 %output_projection.1 = bf16[16,5120]{1,0:T(8,128)(2,1)S(1)} custom-call(bf16[8,16,16,640]{3,2,1,0:T(8,128)(2,1)} %copy-done, bf16[16,64]{1,0:T(8,128)(2,1)S(1)} %fusion.select_ref, bf16[16,512,128]{2,1,0:T(8,128)(2,1)} %value_hbm.1, bf16[2048,5120]{1,0:T(8,128)(2,1)} %weight_hbm.1), custom_call_target="tpu_custom_call" | custom-call | tf_op jit(solution)/shard_map/output_projection/pallas_call | solution.py:319
  136.9 0.7 copy.16
  (5 shorter events, 0.0 us)
Async XLA Ops:
  7.2 29.5 %all-gather.5.cloned.1.call-start = ((), (), s32[]{:S(2)}) async-start(), calls=%async_computation | async-start | bytes 1327104 | tf_op jit(solution)/shard_map/all_gather | solution.py:364
  7.9 60.9 %all-gather.7.cloned.1.call-start = ((), (), s32[]{:S(2)}) async-start(), calls=%async_computation.1 | async-start | bytes 2949120 | tf_op jit(solution)/shard_map/all_gather | solution.py:365
  36.7 2.3 %copy-start.5 = (bf16[128,32,576]{0,2,1:T(8,128)(2,1)S(1)}, bf16[128,32,576]{0,2,1:T(8,128)(2,1)}, u32[]{:S(2)}) copy-start(bf16[128,32,576]{0,2,1:T(8,128)(2,1)} %param.12) | copy-start | bytes 14155780
  39.0 1.3 copy-start.6
  40.3 0.7 copy-start.7
  62.4 6.3 %copy-start.2 = (bf16[16,576]{1,0:T(8,128)(2,1)S(1)}, bf16[16,576]{1,0:T(8,128)(2,1)}, u32[]{:S(2)}) copy-start(bf16[16,576]{1,0:T(8,128)(2,1)} %own_ref.1) | copy-start | bytes 55300
  62.4 6.3 %copy-start.3 = (s32[512]{0:T(512)S(1)}, s32[512]{0:T(512)}, u32[]{:S(2)}) copy-start(s32[512]{0:T(512)} %order_ref.1) | copy-start | bytes 6148
  62.5 6.3 %copy-start.4 = (s32[64]{0:T(128)S(1)}, s32[64]{0:T(128)}, u32[]{:S(2)}) copy-start(s32[64]{0:T(128)} %lengths_ref.3) | copy-start | bytes 772
  68.8 1.7 %copy-start.1 = (bf16[128,16,576]{2,1,0:T(8,128)(2,1)S(1)}, bf16[128,16,576]{2,1,0:T(8,128)(2,1)}, u32[]{:S(2)}) copy-start(bf16[128,16,576]{2,1,0:T(8,128)(2,1)} %all-gather.7.cloned.1.call-done) | copy-start | bytes 7077892
  82.6 1.5 %copy-start = (bf16[8,16,16,640]{3,2,1,0:T(8,128)(2,1)}, bf16[8,16,16,640]{3,2,1,0:T(8,128)(2,1)S(1)}, u32[]{:S(2)}) copy-start(bf16[8,16,16,640]{3,2,1,0:T(8,128)(2,1)S(1)} %decode_attention.1.part_ref) | copy-start | bytes 7864324
Sparse Core Ops, SparseCore 0:
  9.9 26.7 all-gather.4
  38.6 30.1 all-gather.6

commit v2 on v1

--- a/solution.py
+++ b/solution.py
@@ -12,12 +12,74 @@
 VHEAD = 128
 PPR = 8
 STAT = 128
+LISTS = 4
 
 big_negative = -1e30
 log2_e = 1.4426950408889634
 score_scale = (VHEAD + ROPE) ** (-0.5) * log2_e
 f32 = jnp.float32
 bf16 = jnp.bfloat16
+
+
+def gather_kernel(n_seq, block_ref, out_ref, send_chip, recv_chip, send_mate, recv_mate):
+    chips = n_seq // 2
+    seq = lax.axis_index("seq")
+    head = lax.axis_index("head")
+    chip, core = seq // 2, lax.rem(seq, 2)
+    mate = chip * 2 + 1 - core
+
+    def peer(d):
+        return lax.rem(chip + d, chips) * 2 + core
+
+    barrier = pltpu.get_barrier_semaphore()
+    for other in [mate] + [peer(d) for d in range(1, chips)]:
+        pl.semaphore_signal(
+            barrier, inc=1, device_id=(other, head), device_id_type=pl.DeviceIdType.MESH
+        )
+    pl.semaphore_wait(barrier, chips)
+
+    def send(source, slot, other, send_sem, recv_sem):
+        copy = pltpu.make_async_remote_copy(
+            src_ref=source,
+            dst_ref=out_ref.at[slot],
+            send_sem=send_sem,
+            recv_sem=recv_sem,
+            device_id=(other, head),
+            device_id_type=pl.DeviceIdType.MESH,
+        )
+        copy.start()
+        return copy
+
+    over_chips = [
+        send(block_ref, seq, peer(d), send_chip.at[d], recv_chip.at[d]) for d in range(1, chips)
+    ]
+    over_cores = [send(block_ref, seq, mate, send_mate.at[0], recv_mate.at[0])]
+    out_ref[seq] = block_ref[...]
+    for d in range(1, chips):
+        over_chips[d - 1].wait()
+        slot = lax.rem(chip + chips - d, chips) * 2 + core
+        over_cores.append(
+            send(out_ref.at[slot], slot, mate, send_mate.at[d], recv_mate.at[d])
+        )
+    for copy in over_cores:
+        copy.wait()
+
+
+def gather_latents(block, n_seq):
+    vmem = pl.BlockSpec(memory_space=pltpu.VMEM)
+    dma = pltpu.SemaphoreType.DMA
+    chips = n_seq // 2
+    return pl.pallas_call(
+        functools.partial(gather_kernel, n_seq),
+        in_specs=[vmem],
+        out_specs=vmem,
+        out_shape=jax.ShapeDtypeStruct((n_seq, *block.shape), block.dtype),
+        scratch_shapes=[dma((chips,)), dma((chips,)), dma((chips,)), dma((chips,))],
+        compiler_params=pltpu.CompilerParams(
+            collective_id=0, has_side_effects=True, vmem_limit_bytes=16 << 20
+        ),
+        name="latents_gather",
+    )(block)
 
 
 def prefill_kernel(lengths_ref, q_ref, kt_ref, out_ref, bias, keys, keys_t, queries):
@@ -74,7 +136,7 @@
             pltpu.VMEM((width, total), bf16),
             pltpu.VMEM((step * rows, width), bf16),
         ],
-        compiler_params=pltpu.CompilerParams(vmem_limit_bytes=40 << 20),
+        compiler_params=pltpu.CompilerParams(vmem_limit_bytes=56 << 20),
         cost_estimate=pl.CostEstimate(
             flops=2 * heads * rows * total * (width + LAT),
             bytes_accessed=2 * heads * rows * (width + LAT),
@@ -85,7 +147,34 @@
     return jnp.transpose(out, (1, 0, 2))
 
 
-def decode_kernel(order_ref, lengths_ref, q_ref, own_ref, cache_ref, out_ref, top, total, acc, todo):
+def stat_of(level, lane):
+    high = level.astype(bf16).astype(f32)
+    middle = (level - high).astype(bf16).astype(f32)
+    low = level - high - middle
+    return jnp.where(lane == 0, high, jnp.where(lane == 1, middle, low)).astype(bf16)
+
+
+def level_of(x):
+    return (
+        x[..., LAT : LAT + 1].astype(f32)
+        + x[..., LAT + 1 : LAT + 2].astype(f32)
+        + x[..., LAT + 2 : LAT + 3].astype(f32)
+    )
+
+
+def merge(pieces):
+    levels = [level_of(x) for x in pieces]
+    top = functools.reduce(jnp.maximum, levels)
+    shares = [jnp.exp2(level - top) for level in levels]
+    total = functools.reduce(jnp.add, shares)
+    mixed = functools.reduce(
+        jnp.add, [share / total * x[..., :LAT].astype(f32) for share, x in zip(shares, pieces)]
+    )
+    return mixed, top + jnp.log2(total)
+
+
+def decode_kernel(order_ref, lengths_ref, q_ref, own_ref, cache_ref, out_ref, todo, *scratch):
+    top, total, acc = (scratch[i * LISTS : (i + 1) * LISTS] for i in range(3))
     n_seq, rows, heads, width = q_ref.shape
     pages, page = cache_ref.shape[:2]
     all_heads = n_seq * heads
@@ -99,66 +188,77 @@
         def _():
             q = q_ref[:, r].reshape(all_heads, width).astype(f32)
             own = own_ref[r : r + 1, :].astype(f32)
-            top[r] = jnp.sum(q * own, axis=1, keepdims=True) * score_scale
-            total[r] = jnp.ones((all_heads, 1), f32)
-            acc[r] = jnp.broadcast_to(own[:, :LAT], (all_heads, LAT))
+            top[r % LISTS][r // LISTS] = jnp.sum(q * own, axis=1, keepdims=True) * score_scale
+            total[r % LISTS][r // LISTS] = jnp.ones((all_heads, 1), f32)
+            acc[r % LISTS][r // LISTS] = jnp.broadcast_to(own[:, :LAT], (all_heads, LAT))
 
         @pl.when(jnp.logical_not(mine))
         def _():
-            top[r] = jnp.full((all_heads, 1), big_negative, f32)
-            total[r] = jnp.zeros((all_heads, 1), f32)
-            acc[r] = jnp.zeros((all_heads, LAT), f32)
-
-    def collect(i, count):
+            top[r % LISTS][r // LISTS] = jnp.full((all_heads, 1), big_negative, f32)
+            total[r % LISTS][r // LISTS] = jnp.zeros((all_heads, 1), f32)
+            acc[r % LISTS][r // LISTS] = jnp.zeros((all_heads, LAT), f32)
+
+    def collect(i, counts):
         r = i // PPR
         place = order_ref[first * PPR + i]
         limit = lengths_ref[first + r] - (i % PPR) * page
-        use = (place // pages == seq) & (limit > 0)
-        todo[0, count] = r
-        todo[1, count] = place % pages
-        todo[2, count] = limit
-        return count + use.astype(jnp.int32)
-
-    count = lax.fori_loop(0, rows * PPR, collect, jnp.int32(0))
-
-    def one(i, carry):
-        r = todo[0, i]
-        keys = cache_ref[todo[1, i]]
-        q = q_ref[:, r].reshape(all_heads, width)
-        scores = (
-            lax.dot_general(q, keys, (((1,), (1,)), ((), ())), preferred_element_type=f32)
-            * score_scale
-        )
-        spot = lax.broadcasted_iota(jnp.int32, scores.shape, 1)
-        scores = jnp.where(spot < todo[2, i], scores, big_negative)
-        before = top[r]
-        now = jnp.maximum(before, jnp.max(scores, axis=1, keepdims=True))
-        keep = jnp.exp2(before - now)
-        weights = jnp.exp2(scores - now).astype(bf16)
-        top[r] = now
-        total[r] = total[r] * keep + jnp.sum(weights.astype(f32), axis=1, keepdims=True)
-        acc[r] = acc[r] * keep + jnp.dot(weights, keys[:, :LAT], preferred_element_type=f32)
+        use = ((place // pages == seq) & (limit > 0)).astype(jnp.int32)
+        lane = lax.rem(r, LISTS)
+        count = functools.reduce(
+            jnp.add, [jnp.where(lane == n, counts[n], 0) for n in range(LISTS)]
+        )
+        todo[lane * 3, count] = r // LISTS
+        todo[lane * 3 + 1, count] = place % pages
+        todo[lane * 3 + 2, count] = limit
+        return tuple(counts[n] + jnp.where(lane == n, use, 0) for n in range(LISTS))
+
+    counts = lax.fori_loop(0, rows * PPR, collect, (jnp.int32(0),) * LISTS)
+
+    def step(i, carry):
+        state = []
+        for n in range(LISTS):
+            here = i < counts[n]
+            r = jnp.where(here, todo[n * 3, i], 0)
+            keys = cache_ref[jnp.where(here, todo[n * 3 + 1, i], 0)]
+            limit = jnp.where(here, todo[n * 3 + 2, i], 0)
+            q = q_ref[:, r * LISTS + n].reshape(all_heads, width)
+            scores = lax.dot_general(
+                q, keys, (((1,), (1,)), ((), ())), preferred_element_type=f32
+            )
+            state.append((r, keys, limit, scores * score_scale))
+        for n, (r, keys, limit, scores) in enumerate(state):
+            valid = lax.broadcasted_iota(jnp.int32, scores.shape, 1) < limit
+            scores = jnp.where(valid, scores, big_negative)
+            before = top[n][r]
+            now = jnp.maximum(before, jnp.max(scores, axis=1, keepdims=True))
+            keep = jnp.exp2(before - now)
+            weights = jnp.where(valid, jnp.exp2(scores - now), 0.0).astype(bf16)
+            top[n][r] = now
+            total[n][r] = total[n][r] * keep + jnp.sum(
+                weights.astype(f32), axis=1, keepdims=True
+            )
+            acc[n][r] = acc[n][r] * keep + jnp.dot(
+                weights, keys[:, :LAT], preferred_element_type=f32
+            )
         return carry
 
-    lax.fori_loop(0, count, one, 0)
+    lax.fori_loop(0, functools.reduce(jnp.maximum, counts), step, 0)
 
     lane = lax.broadcasted_iota(jnp.int32, (all_heads, STAT), 1)
 
-    def finish(r, carry):
-        sums = total[r]
-        some = sums > 0
-        sums = jnp.where(some, sums, 1.0)
-        mixed = (acc[r] / sums).astype(bf16)
-        level = jnp.where(some, top[r] + jnp.log2(sums), big_negative)
-        high = level.astype(bf16).astype(f32)
-        middle = (level - high).astype(bf16).astype(f32)
-        low = level - high - middle
-        stat = jnp.where(lane == 0, high, jnp.where(lane == 1, middle, low)).astype(bf16)
-        out_ref[:, r, :, :LAT] = mixed.reshape(n_seq, heads, LAT)
-        out_ref[:, r, :, LAT:] = stat.reshape(n_seq, heads, STAT)
+    def finish(i, carry):
+        for n in range(LISTS):
+            r = i * LISTS + n
+            sums = total[n][i]
+            some = sums > 0
+            sums = jnp.where(some, sums, 1.0)
+            mixed = (acc[n][i] / sums).astype(bf16)
+            level = jnp.where(some, top[n][i] + jnp.log2(sums), big_negative)
+            out_ref[:, r, :, :LAT] = mixed.reshape(n_seq, heads, LAT)
+            out_ref[:, r, :, LAT:] = stat_of(level, lane).reshape(n_seq, heads, STAT)
         return carry
 
-    lax.fori_loop(0, rows, finish, 0)
+    lax.fori_loop(0, rows // LISTS, finish, 0)
 
 
 def decode(page_order, dec_lengths, queries, own_latents, cache_pages):
@@ -171,10 +271,9 @@
         out_specs=vmem,
         out_shape=jax.ShapeDtypeStruct((n_seq, rows, heads, LAT + STAT), bf16),
         scratch_shapes=[
-            pltpu.VMEM((rows, n_seq * heads, 1), f32),
-            pltpu.VMEM((rows, n_seq * heads, 1), f32),
-            pltpu.VMEM((rows, n_seq * heads, LAT), f32),
-            pltpu.SMEM((3, rows * PPR + 1), jnp.int32),
+            pltpu.SMEM((3 * LISTS, rows // LISTS * PPR + 1), jnp.int32),
+            *[pltpu.VMEM((rows // LISTS, n_seq * heads, 1), f32) for _ in range(2 * LISTS)],
+            *[pltpu.VMEM((rows // LISTS, n_seq * heads, LAT), f32) for _ in range(LISTS)],
         ],
         compiler_params=pltpu.CompilerParams(vmem_limit_bytes=48 << 20),
         name="decode_attention",
@@ -183,8 +282,8 @@
 
 def tail_kernel(
     n_seq, n_head, part_ref, select_ref, value_hbm, weight_hbm, out_ref,
-    got, mixed, values, value, weight, sums_out, sums_in, final, zrows, chosen, gathered,
-    local_sem, send_a, recv_a, send_b, recv_b, send_c, recv_c, send_d, recv_d,
+    from_mate, merged, got, mixed, values, value, weight, sums_out, sums_in, final, zrows, chosen, gathered,
+    local_sem, send_m, recv_m, send_a, recv_a, send_b, recv_b, send_c, recv_c, send_d, recv_d,
 ):
     rows = part_ref.shape[1]
     heads = part_ref.shape[2]
@@ -235,30 +334,46 @@
         copy.start()
         return copy
 
-    first = [
-        to_seq(part_ref.at[seq_peer(d)], got.at[d], send_a, recv_a, d) for d in range(1, n_seq)
-    ]
+    chips = n_seq // 2
+    chip, core = seq // 2, lax.rem(seq, 2)
+    mate = chip * 2 + 1 - core
+
+    def chip_of(d):
+        return lax.rem(chip + d, chips)
+
+    def to(source, target, send_sem, recv_sem, other):
+        copy = pltpu.make_async_remote_copy(
+            src_ref=source,
+            dst_ref=target,
+            send_sem=send_sem,
+            recv_sem=recv_sem,
+            device_id=(other, head),
+            device_id_type=pl.DeviceIdType.MESH,
+        )
+        copy.start()
+        return copy
+
+    order = list(range(1, chips)) + [0]
+    zeroth = {
+        d: to(
+            part_ref.at[chip_of(d) * 2 + 1 - core], from_mate.at[d], send_m.at[d], recv_m.at[d], mate
+        )
+        for d in order
+    }
+    lane = lax.broadcasted_iota(jnp.int32, (rows, heads, STAT), 2)
+    first = []
+    for d in order:
+        zeroth[d].wait()
+        both, level = merge([part_ref[chip_of(d) * 2 + core], from_mate[d]])
+        merged[d, :, :, :LAT] = both.astype(bf16)
+        merged[d, :, :, LAT:] = stat_of(level, lane)
+        if d:
+            first.append(
+                to(merged.at[d], got.at[d], send_a.at[d], recv_a.at[d], chip_of(d) * 2 + core)
+            )
     for copy in first:
         copy.wait()
-
-    def piece(d):
-        return part_ref[seq] if d == 0 else got[d]
-
-    def level_of(x):
-        return (
-            x[:, :, LAT : LAT + 1].astype(f32)
-            + x[:, :, LAT + 1 : LAT + 2].astype(f32)
-            + x[:, :, LAT + 2 : LAT + 3].astype(f32)
-        )
-
-    levels = [level_of(piece(d)) for d in range(n_seq)]
-    top = functools.reduce(jnp.maximum, levels)
-    shares = [jnp.exp2(level - top) for level in levels]
-    total = functools.reduce(jnp.add, shares)
-    result = jnp.zeros((rows, heads, LAT), f32)
-    for d in range(n_seq):
-        result = result + (shares[d] / total) * piece(d)[:, :, :LAT].astype(f32)
-    mixed[...] = result
+    mixed[...] = merge([merged[0]] + [got[d] for d in range(1, chips)])[0]
 
     value_copy.wait()
     for h in range(heads):
@@ -322,7 +437,9 @@
         out_specs=vmem,
         out_shape=jax.ShapeDtypeStruct((rows, width), bf16),
         scratch_shapes=[
-            pltpu.VMEM((n_seq, rows, heads, wide), bf16),
+            pltpu.VMEM((n_seq // 2, rows, heads, wide), bf16),
+            pltpu.VMEM((n_seq // 2, rows, heads, wide), bf16),
+            pltpu.VMEM((n_seq // 2, rows, heads, wide), bf16),
             pltpu.VMEM((rows, heads, LAT), f32),
             pltpu.VMEM((rows, depth), bf16),
             pltpu.VMEM(value_up.shape, bf16),
@@ -334,13 +451,14 @@
             pltpu.VMEM((rows, chunk), bf16),
             pltpu.VMEM((n_seq, rows, chunk), bf16),
             dma((owners + 1,)),
-            dma((n_seq,)), dma((n_seq,)),
+            dma((n_seq // 2,)), dma((n_seq // 2,)),
+            dma((n_seq // 2,)), dma((n_seq // 2,)),
             dma((n_seq,)), dma((n_seq,)),
             dma((n_head,)), dma((n_head,)),
             dma((n_seq,)), dma((n_seq,)),
         ],
         compiler_params=pltpu.CompilerParams(
-            collective_id=1, has_side_effects=True, vmem_limit_bytes=52 << 20
+            collective_id=1, has_side_effects=True, vmem_limit_bytes=42 << 20
         ),
         name="output_projection",
     )(part, select, value_up, out_weight)
@@ -361,8 +479,8 @@
 ):
     n_head = lax.axis_size("head")
     rows = dec_queries.shape[0]
-    latents_t = lax.all_gather(prefill_latents.T, "seq", axis=0)
     queries = lax.all_gather(dec_queries, "seq", axis=0)
+    latents_t = gather_latents(prefill_latents.T, lax.axis_size("seq"))
     prefill_out = prefill(prompt_lengths, prefill_queries, latents_t)
     part = decode(page_order, dec_lengths, queries, dec_new_latent, cache_pages)
     members = lax.dynamic_slice_in_dim(group_members, lax.axis_index("head") * rows, rows)

time: 145 us -> 116 us (0.80)
  waiting for transfers between devices: 30.5 us -> 0.68 us
  Pallas kernels: 86.4 us -> 89.4 us
  local copies, waits for them, and re-layouts: 13.3 us -> 11 us
    all_gather x1 -> x0, waiting for transfers between devices: 27.2 us -> none  [on_device(): latents_t = lax.all_gather(prefill_latents.T, 'seq', axis=0)]
    pallas_call x0 -> x1, Pallas kernels: none -> 12.5 us  [gather_latents(): pl.pallas_call(functools.partial(gather_kernel, n_seq), in_specs=[vmem],...]
    pallas_call x1, Pallas kernels: 52.8 us -> 40.3 us  [tail(): pl.pallas_call(functools.partial(tail_kernel, n_seq, n_head), in_specs=[v...]
    all_gather x1, waiting for transfers between devices: 1.92 us -> 0.01 us  [on_device(): queries = lax.all_gather(dec_queries, 'seq', axis=0)]
    unnamed x18, local copies, waits for them, and re-layouts: 12.6 us -> 10.9 us
    pallas_call x1, Pallas kernels: 12.1 us -> 13.6 us  [decode(): pl.pallas_call(decode_kernel, in_specs=[smem, smem, vmem, vmem, vmem], ou...]
    pallas_call x1, Pallas kernels: 21.5 us -> 23 us  [prefill(): pl.pallas_call(prefill_kernel, grid=(heads // step,), in_specs=[pl.BlockS...]
  transfers between devices with their start and end apart: 2 -> 1, of which waited for: 2 -> 0; matrix products, arithmetic and copies ran while one was open for 4% -> 6% of each run, Pallas kernels for 15% -> 31%
where the time goes in v2:
time: 116 us; the launch traced here: 115 us
  Pallas kernels  89.4 us (77%)
  between operations  14.1 us (12%)
  local copies, waits for them, and re-layouts  11 us (9%)
    pallas_call x1, Pallas kernels, tail(): pl.pallas_call(functools.partial(tail_kernel, n_seq, n_head), in_specs=[v...  40.3 us
    pallas_call x1, Pallas kernels, prefill(): pl.pallas_call(prefill_kernel, grid=(heads // step,), in_specs=[pl.BlockS...  23 us
    pallas_call x1, Pallas kernels, decode(): pl.pallas_call(decode_kernel, in_specs=[smem, smem, vmem, vmem, vmem], ou...  13.6 us
    pallas_call x1, Pallas kernels, gather_latents(): pl.pallas_call(functools.partial(gather_kernel, n_seq), in_specs=[vmem],...  12.5 us
    unnamed x18, local copies, waits for them, and re-layouts  10.9 us
  transfers between devices with their start and end apart: 1, of which 0 were waited for; matrix products, arithmetic and copies ran while one was open for 6% of the time, Pallas kernels for 31%

profile of v2, /device:TPU:0, one launch (start us, length us, event | category | flops | bytes accessed | tf_op | source)
XLA Modules:
  0.0 115.3 jit_solution(4507083720360568994)
XLA Ops:
  7.2 0.0 all-gather.3.cloned.1.call-start
  7.2 0.7 all-gather.3.cloned.1.call-update
  7.9 0.0 copy-start.3
  7.9 0.9 copy-done.3
  8.8 12.5 %latents_gather.1.kt_ref = bf16[8,576,128]{2,1,0:T(8,128)(2,1)S(1)} custom-call(bf16[576,128]{1,0:T(8,128)(2,1)S(1)} %bitcast.5), custom_call_target="tpu_custom_call" | custom-call | tf_op jit(solution)/shard_map/latents_gather/pallas_call | solution.py:72
  21.4 0.0 copy-start.2
  21.4 1.0 copy-done.2
  22.4 23.0 %prefill_attention.1 = bf16[32,128,512]{2,1,0:T(8,128)(2,1)} custom-call(s32[4]{0:T(128)} %lengths_ref.2, bf16[32,576,128]{2,1,0:T(8,128)(2,1)} %bitcast.7, bf16[8,576,128]{2,1,0:T(8,128)(2,1)} %copy-done.2), custom_call_target="tpu_custom_call" | custom-call | flops 9126805504 | bytes 8912896 | tf_op jit(solution)/shard_map/prefill_attention/pallas_call | solution.py:123
  45.3 0.0 copy-start.7
  45.3 0.0 copy-start.4
  45.3 0.0 copy-start.6
  45.4 6.6 %copy.14 = bf16[128,32,512]{2,1,0:T(8,128)(2,1)} copy(bf16[128,32,512]{2,0,1:T(8,128)(2,1)} %bitcast.6) | data formatting | bytes 8388608
  51.9 0.0 copy-done.7
  51.9 0.1 dynamic_slice.3
  52.0 0.1 fusion.select_ref
  52.1 0.0 copy-done.4
  52.1 0.0 copy-done.5
  52.1 0.0 copy-done.6
  52.1 0.0 copy-start
  52.1 1.7 %copy-done = bf16[128,16,576]{2,1,0:T(8,128)(2,1)S(1)} copy-done((bf16[128,16,576]{2,1,0:T(8,128)(2,1)S(1)}, bf16[128,16,576]{2,1,0:T(8,128)(2,1)}, u32[]{:S(2)}) %copy-start) | copy-done | bytes 2359320
  53.9 13.6 %decode_attention.1.part_ref = bf16[8,16,16,640]{3,2,1,0:T(8,128)(2,1)S(1)} custom-call(s32[512]{0:T(512)S(1)} %copy-done.5, s32[64]{0:T(128)S(1)} %copy-done.6, bf16[8,16,16,576]{3,2,1,0:T(8,128)(2,1)S(1)} %bitcast.4, bf16[16,576]{1,0:T(8,128)(2,1)S(1)} %copy-done.4, bf16[64,64,576]{2,1,0:T(8,128)(2,1)} %cache_ref.1), custom_call_target="tpu_custom_call" | custom-call | tf_op jit(solution)/shard_map/decode_attention/pallas_call | solution.py:268
  67.5 0.0 copy-done.1
  67.5 40.3 %output_projection.1 = bf16[16,5120]{1,0:T(8,128)(2,1)S(1)} custom-call(bf16[8,16,16,640]{3,2,1,0:T(8,128)(2,1)S(1)} %decode_attention.1.part_ref, bf16[16,64]{1,0:T(8,128)(2,1)S(1)} %fusion.select_ref, bf16[16,512,128]{2,1,0:T(8,128)(2,1)S(1)} %copy-done.1, bf16[2048,5120]{1,0:T(8,128)(2,1)} %weight_hbm.1), custom_call_target="tpu_custom_call" | custom-call | tf_op jit(solution)/shard_map/output_projection/pallas_call | solution.py:434
  107.8 0.7 copy.16
  (3 shorter events, 0.0 us)
Async XLA Ops:
  7.2 44.9 %all-gather.3.cloned.1.call-start = ((), (), s32[]{:S(2)}) async-start(), calls=%async_computation | async-start | bytes 2949120 | tf_op jit(solution)/shard_map/all_gather | solution.py:482
  7.9 0.9 copy-start.3
  21.4 1.0 copy-start.2
  45.3 6.6 %copy-start.7 = (s32[64]{0:T(128)S(1)}, s32[64]{0:T(128)}, u32[]{:S(2)}) copy-start(s32[64]{0:T(128)} %param.14) | copy-start | bytes 772
  45.3 6.8 %copy-start.4 = (bf16[16,576]{1,0:T(8,128)(2,1)S(1)}, bf16[16,576]{1,0:T(8,128)(2,1)}, u32[]{:S(2)}) copy-start(bf16[16,576]{1,0:T(8,128)(2,1)} %own_ref.1) | copy-start | bytes 55300
  45.3 6.8 %copy-start.5 = (s32[512]{0:T(512)S(1)}, s32[512]{0:T(512)}, u32[]{:S(2)}) copy-start(s32[512]{0:T(512)} %order_ref.1) | copy-start | bytes 6148
  45.3 6.8 %copy-start.6 = (s32[64]{0:T(128)S(1)}, s32[64]{0:T(128)}, u32[]{:S(2)}) copy-start(s32[64]{0:T(128)} %lengths_ref.3) | copy-start | bytes 772
  52.1 1.7 %copy-start = (bf16[128,16,576]{2,1,0:T(8,128)(2,1)S(1)}, bf16[128,16,576]{2,1,0:T(8,128)(2,1)}, u32[]{:S(2)}) copy-start(bf16[128,16,576]{2,1,0:T(8,128)(2,1)} %all-gather.3.cloned.1.call-done) | copy-start | bytes 7077892
  53.9 13.6 %copy-start.1 = (bf16[16,512,128]{2,1,0:T(8,128)(2,1)S(1)}, bf16[16,512,128]{2,1,0:T(8,128)(2,1)}, u32[]{:S(2)}) copy-start(bf16[16,512,128]{2,1,0:T(8,128)(2,1)} %value_hbm.1) | copy-start | bytes 6291460
Sparse Core Ops, SparseCore 0:
  9.9 32.8 all-gather.2

commit v3 on v2

--- a/solution.py
+++ b/solution.py
@@ -21,7 +21,9 @@
 bf16 = jnp.bfloat16
 
 
-def gather_kernel(n_seq, block_ref, out_ref, send_chip, recv_chip, send_mate, recv_mate):
+def gather_kernel(n_seq, *refs):
+    pairs = ((refs[0], refs[2]), (refs[1], refs[3]))
+    send_chip, recv_chip, send_mate, recv_mate = refs[4:]
     chips = n_seq // 2
     seq = lax.axis_index("seq")
     head = lax.axis_index("head")
@@ -38,10 +40,10 @@
         )
     pl.semaphore_wait(barrier, chips)
 
-    def send(source, slot, other, send_sem, recv_sem):
+    def send(source, target, other, send_sem, recv_sem):
         copy = pltpu.make_async_remote_copy(
             src_ref=source,
-            dst_ref=out_ref.at[slot],
+            dst_ref=target,
             send_sem=send_sem,
             recv_sem=recv_sem,
             device_id=(other, head),
@@ -50,46 +52,80 @@
         copy.start()
         return copy
 
-    over_chips = [
-        send(block_ref, seq, peer(d), send_chip.at[d], recv_chip.at[d]) for d in range(1, chips)
-    ]
-    over_cores = [send(block_ref, seq, mate, send_mate.at[0], recv_mate.at[0])]
-    out_ref[seq] = block_ref[...]
-    for d in range(1, chips):
-        over_chips[d - 1].wait()
-        slot = lax.rem(chip + chips - d, chips) * 2 + core
-        over_cores.append(
-            send(out_ref.at[slot], slot, mate, send_mate.at[d], recv_mate.at[d])
-        )
+    over_chips = {
+        (p, d): send(block, out.at[seq], peer(d), send_chip.at[p, d], recv_chip.at[p, d])
+        for p, (block, out) in enumerate(pairs)
+        for d in range(1, chips)
+    }
+    over_cores = []
+    for p, (block, out) in enumerate(pairs):
+        over_cores.append(send(block, out.at[seq], mate, send_mate.at[p, 0], recv_mate.at[p, 0]))
+        out[seq] = block[...]
+    for p, (block, out) in enumerate(pairs):
+        for d in range(1, chips):
+            over_chips[p, d].wait()
+            slot = lax.rem(chip + chips - d, chips) * 2 + core
+            over_cores.append(
+                send(out.at[slot], out.at[slot], mate, send_mate.at[p, d], recv_mate.at[p, d])
+            )
     for copy in over_cores:
         copy.wait()
 
 
-def gather_latents(block, n_seq):
+def gather(blocks, n_seq):
     vmem = pl.BlockSpec(memory_space=pltpu.VMEM)
-    dma = pltpu.SemaphoreType.DMA
-    chips = n_seq // 2
+    dma = pltpu.SemaphoreType.DMA((2, n_seq // 2))
     return pl.pallas_call(
         functools.partial(gather_kernel, n_seq),
-        in_specs=[vmem],
-        out_specs=vmem,
-        out_shape=jax.ShapeDtypeStruct((n_seq, *block.shape), block.dtype),
-        scratch_shapes=[dma((chips,)), dma((chips,)), dma((chips,)), dma((chips,))],
+        in_specs=[vmem, vmem],
+        out_specs=[vmem, vmem],
+        out_shape=[jax.ShapeDtypeStruct((n_seq, *x.shape), x.dtype) for x in blocks],
+        scratch_shapes=[dma, dma, dma, dma],
         compiler_params=pltpu.CompilerParams(
             collective_id=0, has_side_effects=True, vmem_limit_bytes=16 << 20
         ),
-        name="latents_gather",
-    )(block)
-
-
-def prefill_kernel(lengths_ref, q_ref, kt_ref, out_ref, bias, keys, keys_t, queries):
+        name="gather_over_seq",
+    )(*blocks)
+
+
+def prefill_kernel(
+    lengths_ref, q_ref, kt_ref, part_ref, out_ref, got_ref,
+    bias, keys, keys_t, queries, send_sem, recv_sem, own_sem,
+):
     blocks, width, rows = kt_ref.shape
     total = blocks * rows
     heads = q_ref.shape[0]
+    seq = lax.axis_index("seq")
+    head = lax.axis_index("head")
+
+    def exchange():
+        own = pltpu.make_async_copy(part_ref.at[seq], got_ref.at[0], own_sem)
+        return [own] + [
+            pltpu.make_async_remote_copy(
+                src_ref=part_ref.at[lax.rem(seq + d, blocks)],
+                dst_ref=got_ref.at[d],
+                send_sem=send_sem.at[d],
+                recv_sem=recv_sem.at[d],
+                device_id=(lax.rem(seq + d, blocks), head),
+                device_id_type=pl.DeviceIdType.MESH,
+            )
+            for d in range(1, blocks)
+        ]
 
     @pl.when(pl.program_id(0) == 0)
     def _():
-        t = lax.broadcasted_iota(jnp.int32, (rows, total), 0) + lax.axis_index("seq") * rows
+        barrier = pltpu.get_barrier_semaphore()
+        for d in range(1, blocks):
+            pl.semaphore_signal(
+                barrier,
+                inc=1,
+                device_id=(lax.rem(seq + d, blocks), head),
+                device_id_type=pl.DeviceIdType.MESH,
+            )
+        pl.semaphore_wait(barrier, blocks - 1)
+        for copy in exchange():
+            copy.start()
+        t = lax.broadcasted_iota(jnp.int32, (rows, total), 0) + seq * rows
         k = lax.broadcasted_iota(jnp.int32, (rows, total), 1)
         bound = jnp.int32(0)
         start = jnp.zeros((rows, total), jnp.int32)
@@ -109,42 +145,59 @@
         )
         scores = scores * score_scale + bias[...]
         top = jnp.max(scores, axis=1, keepdims=True)
-        weights = jnp.exp2(scores - top).astype(bf16)
-        sums = jnp.sum(weights.astype(f32), axis=1, keepdims=True)
-        mixed = jnp.dot(weights, keys[...], preferred_element_type=f32)
-        out_ref[h] = (mixed / sums).astype(bf16)
-
-
-def prefill(prompt_lengths, queries, latents_t):
+        weights = jnp.exp2(scores - top)
+        sums = jnp.sum(weights, axis=1, keepdims=True)
+        mixed = jnp.dot(weights.astype(bf16), keys[...], preferred_element_type=f32)
+        out_ref[h] = (mixed * (1.0 / sums)).astype(bf16)
+
+    @pl.when(pl.program_id(0) == pl.num_programs(0) - 1)
+    def _():
+        for copy in exchange():
+            copy.wait()
+
+
+def prefill(prompt_lengths, queries, latents_t, part):
     rows, heads, width = queries.shape
     blocks = latents_t.shape[0]
     step = max(1, 512 // rows)
     total = blocks * rows
-    out = pl.pallas_call(
+    out, got = pl.pallas_call(
         prefill_kernel,
         grid=(heads // step,),
         in_specs=[
             pl.BlockSpec(memory_space=pltpu.SMEM),
             pl.BlockSpec((step, width, rows), lambda i: (i, 0, 0)),
             pl.BlockSpec((blocks, width, rows), lambda i: (0, 0, 0)),
+            pl.BlockSpec(memory_space=pl.ANY),
         ],
-        out_specs=pl.BlockSpec((step, rows, LAT), lambda i: (i, 0, 0)),
-        out_shape=jax.ShapeDtypeStruct((heads, rows, LAT), bf16),
+        out_specs=[
+            pl.BlockSpec((step, rows, LAT), lambda i: (i, 0, 0)),
+            pl.BlockSpec(memory_space=pl.ANY),
+        ],
+        out_shape=[
+            jax.ShapeDtypeStruct((heads, rows, LAT), bf16),
+            jax.ShapeDtypeStruct(part.shape, part.dtype),
+        ],
         scratch_shapes=[
             pltpu.VMEM((rows, total), f32),
             pltpu.VMEM((total, LAT), bf16),
             pltpu.VMEM((width, total), bf16),
             pltpu.VMEM((step * rows, width), bf16),
+            pltpu.SemaphoreType.DMA((blocks,)),
+            pltpu.SemaphoreType.DMA((blocks,)),
+            pltpu.SemaphoreType.DMA,
         ],
-        compiler_params=pltpu.CompilerParams(vmem_limit_bytes=56 << 20),
+        compiler_params=pltpu.CompilerParams(
+            collective_id=2, has_side_effects=True, vmem_limit_bytes=56 << 20
+        ),
         cost_estimate=pl.CostEstimate(
             flops=2 * heads * rows * total * (width + LAT),
             bytes_accessed=2 * heads * rows * (width + LAT),
             transcendentals=heads * rows * total,
         ),
         name="prefill_attention",
-    )(prompt_lengths, jnp.transpose(queries, (1, 2, 0)), latents_t)
-    return jnp.transpose(out, (1, 0, 2))
+    )(prompt_lengths, jnp.transpose(queries, (1, 2, 0)), latents_t, part)
+    return jnp.transpose(out, (1, 0, 2)), got
 
 
 def stat_of(level, lane):
@@ -170,7 +223,7 @@
     mixed = functools.reduce(
         jnp.add, [share / total * x[..., :LAT].astype(f32) for share, x in zip(shares, pieces)]
     )
-    return mixed, top + jnp.log2(total)
+    return mixed
 
 
 def decode_kernel(order_ref, lengths_ref, q_ref, own_ref, cache_ref, out_ref, todo, *scratch):
@@ -199,20 +252,21 @@
             acc[r % LISTS][r // LISTS] = jnp.zeros((all_heads, LAT), f32)
 
     def collect(i, counts):
-        r = i // PPR
-        place = order_ref[first * PPR + i]
-        limit = lengths_ref[first + r] - (i % PPR) * page
-        use = ((place // pages == seq) & (limit > 0)).astype(jnp.int32)
-        lane = lax.rem(r, LISTS)
-        count = functools.reduce(
-            jnp.add, [jnp.where(lane == n, counts[n], 0) for n in range(LISTS)]
-        )
-        todo[lane * 3, count] = r // LISTS
-        todo[lane * 3 + 1, count] = place % pages
-        todo[lane * 3 + 2, count] = limit
-        return tuple(counts[n] + jnp.where(lane == n, use, 0) for n in range(LISTS))
-
-    counts = lax.fori_loop(0, rows * PPR, collect, (jnp.int32(0),) * LISTS)
+        counts = list(counts)
+        for n in range(LISTS):
+            r = i * LISTS + n
+            length = lengths_ref[first + r]
+            for j in range(PPR):
+                place = order_ref[(first + r) * PPR + j]
+                limit = length - j * page
+                todo[n * 3, counts[n]] = i
+                todo[n * 3 + 1, counts[n]] = lax.rem(place, pages)
+                todo[n * 3 + 2, counts[n]] = limit
+                use = (lax.div(place, pages) == seq) & (limit > 0)
+                counts[n] = counts[n] + use.astype(jnp.int32)
+        return tuple(counts)
+
+    counts = lax.fori_loop(0, rows // LISTS, collect, (jnp.int32(0),) * LISTS)
 
     def step(i, carry):
         state = []
@@ -232,13 +286,11 @@
             before = top[n][r]
             now = jnp.maximum(before, jnp.max(scores, axis=1, keepdims=True))
             keep = jnp.exp2(before - now)
-            weights = jnp.where(valid, jnp.exp2(scores - now), 0.0).astype(bf16)
+            weights = jnp.where(valid, jnp.exp2(scores - now), 0.0)
             top[n][r] = now
-            total[n][r] = total[n][r] * keep + jnp.sum(
-                weights.astype(f32), axis=1, keepdims=True
-            )
+            total[n][r] = total[n][r] * keep + jnp.sum(weights, axis=1, keepdims=True)
             acc[n][r] = acc[n][r] * keep + jnp.dot(
-                weights, keys[:, :LAT], preferred_element_type=f32
+                weights.astype(bf16), keys[:, :LAT], preferred_element_type=f32
             )
         return carry
 
@@ -282,8 +334,8 @@
 
 def tail_kernel(
     n_seq, n_head, part_ref, select_ref, value_hbm, weight_hbm, out_ref,
-    from_mate, merged, got, mixed, values, value, weight, sums_out, sums_in, final, zrows, chosen, gathered,
-    local_sem, send_m, recv_m, send_a, recv_a, send_b, recv_b, send_c, recv_c, send_d, recv_d,
+    mixed, values, value, weight, sums_out, sums_in, final, zrows, chosen, gathered,
+    local_sem, send_b, recv_b, send_c, recv_c, send_d, recv_d,
 ):
     rows = part_ref.shape[1]
     heads = part_ref.shape[2]
@@ -334,46 +386,7 @@
         copy.start()
         return copy
 
-    chips = n_seq // 2
-    chip, core = seq // 2, lax.rem(seq, 2)
-    mate = chip * 2 + 1 - core
-
-    def chip_of(d):
-        return lax.rem(chip + d, chips)
-
-    def to(source, target, send_sem, recv_sem, other):
-        copy = pltpu.make_async_remote_copy(
-            src_ref=source,
-            dst_ref=target,
-            send_sem=send_sem,
-            recv_sem=recv_sem,
-            device_id=(other, head),
-            device_id_type=pl.DeviceIdType.MESH,
-        )
-        copy.start()
-        return copy
-
-    order = list(range(1, chips)) + [0]
-    zeroth = {
-        d: to(
-            part_ref.at[chip_of(d) * 2 + 1 - core], from_mate.at[d], send_m.at[d], recv_m.at[d], mate
-        )
-        for d in order
-    }
-    lane = lax.broadcasted_iota(jnp.int32, (rows, heads, STAT), 2)
-    first = []
-    for d in order:
-        zeroth[d].wait()
-        both, level = merge([part_ref[chip_of(d) * 2 + core], from_mate[d]])
-        merged[d, :, :, :LAT] = both.astype(bf16)
-        merged[d, :, :, LAT:] = stat_of(level, lane)
-        if d:
-            first.append(
-                to(merged.at[d], got.at[d], send_a.at[d], recv_a.at[d], chip_of(d) * 2 + core)
-            )
-    for copy in first:
-        copy.wait()
-    mixed[...] = merge([merged[0]] + [got[d] for d in range(1, chips)])[0]
+    mixed[...] = merge([part_ref[d] for d in range(n_seq)])
 
     value_copy.wait()
     for h in range(heads):
@@ -437,9 +450,6 @@
         out_specs=vmem,
         out_shape=jax.ShapeDtypeStruct((rows, width), bf16),
         scratch_shapes=[
-            pltpu.VMEM((n_seq // 2, rows, heads, wide), bf16),
-            pltpu.VMEM((n_seq // 2, rows, heads, wide), bf16),
-            pltpu.VMEM((n_seq // 2, rows, heads, wide), bf16),
             pltpu.VMEM((rows, heads, LAT), f32),
             pltpu.VMEM((rows, depth), bf16),
             pltpu.VMEM(value_up.shape, bf16),
@@ -451,8 +461,6 @@
             pltpu.VMEM((rows, chunk), bf16),
             pltpu.VMEM((n_seq, rows, chunk), bf16),
             dma((owners + 1,)),
-            dma((n_seq // 2,)), dma((n_seq // 2,)),
-            dma((n_seq // 2,)), dma((n_seq // 2,)),
             dma((n_seq,)), dma((n_seq,)),
             dma((n_head,)), dma((n_head,)),
             dma((n_seq,)), dma((n_seq,)),
@@ -479,10 +487,9 @@
 ):
     n_head = lax.axis_size("head")
     rows = dec_queries.shape[0]
-    queries = lax.all_gather(dec_queries, "seq", axis=0)
-    latents_t = gather_latents(prefill_latents.T, lax.axis_size("seq"))
-    prefill_out = prefill(prompt_lengths, prefill_queries, latents_t)
+    queries, latents_t = gather((dec_queries, prefill_latents.T), lax.axis_size("seq"))
     part = decode(page_order, dec_lengths, queries, dec_new_latent, cache_pages)
+    prefill_out, part = prefill(prompt_lengths, prefill_queries, latents_t, part)
     members = lax.dynamic_slice_in_dim(group_members, lax.axis_index("head") * rows, rows)
     select = jax.nn.one_hot(members, n_head * rows, dtype=bf16)
     dec_out = tail(part, select, value_up, out_weight, n_head)

time: 116 us -> 108 us (0.931)
  between operations: 14.1 us -> 0.71 us
  Pallas kernels: 89.4 us -> 92.7 us
  local copies, waits for them, and re-layouts: 11 us -> 14 us
    pallas_call x1, Pallas kernels: 40.3 us -> 19.8 us  [tail(): pl.pallas_call(functools.partial(tail_kernel, n_seq, n_head), in_specs=[v...]
    pallas_call x1, Pallas kernels: 12.5 us -> 26.7 us  [gather(): pl.pallas_call(functools.partial(gather_kernel, n_seq), in_specs=[vmem, v...]
    pallas_call x1, Pallas kernels: 23 us -> 34.9 us  [prefill(): pl.pallas_call(prefill_kernel, grid=(heads // step,), in_specs=[pl.BlockS...]
    unnamed x18 -> x22, local copies, waits for them, and re-layouts: 10.9 us -> 13.2 us
    pallas_call x1, Pallas kernels: 13.6 us -> 11.3 us  [decode(): pl.pallas_call(decode_kernel, in_specs=[smem, smem, vmem, vmem, vmem], ou...]
  transfers between devices with their start and end apart: 1 -> 0, of which waited for: 0 -> 0; matrix products, arithmetic and copies ran while one was open for 6% -> 0% of each run, Pallas kernels for 31% -> 0%
where the time goes in v3:
time: 108 us; the launch traced here: 107 us
  Pallas kernels  92.7 us (86%)
  local copies, waits for them, and re-layouts  14 us (13%)
    pallas_call x1, Pallas kernels, prefill(): pl.pallas_call(prefill_kernel, grid=(heads // step,), in_specs=[pl.BlockS...  34.9 us
    pallas_call x1, Pallas kernels, gather(): pl.pallas_call(functools.partial(gather_kernel, n_seq), in_specs=[vmem, v...  26.7 us
    pallas_call x1, Pallas kernels, tail(): pl.pallas_call(functools.partial(tail_kernel, n_seq, n_head), in_specs=[v...  19.8 us
    unnamed x22, local copies, waits for them, and re-layouts  13.2 us
    pallas_call x1, Pallas kernels, decode(): pl.pallas_call(decode_kernel, in_specs=[smem, smem, vmem, vmem, vmem], ou...  11.3 us

profile of v3, /device:TPU:0, one launch (start us, length us, event | category | flops | bytes accessed | tf_op | source)
XLA Modules:
  0.0 107.5 jit_solution(4830580167711985382)
XLA Ops:
  0.6 0.7 dynamic_slice.3
  1.4 0.1 fusion.select_ref
  1.4 0.0 copy-start.3
  1.4 1.0 copy-done.3
  2.4 0.0 copy-start.4
  2.4 0.9 copy-done.4
  3.3 26.7 %gather_over_seq.1 = (bf16[8,16,16,576]{3,2,1,0:T(8,128)(2,1)S(1)}, bf16[8,576,128]{2,1,0:T(8,128)(2,1)S(1)}) custom-call(bf16[16,16,576]{2,1,0:T(8,128)(2,1)S(1)} %copy-done.3, bf16[576,128]{1,0:T(8,128)(2,1)S(1)} %bitcast.3), custom_call_target="tpu_custom_call" | custom-call | tf_op jit(solution)/shard_map/gather_over_seq/pallas_call | solution.py:78
  30.1 0.0 copy-start.8
  30.1 1.0 copy-done.8
  31.1 0.0 copy-start.5
  31.1 0.7 copy-done.5
  31.8 0.7 copy-done.6
  32.5 0.7 copy-done.7
  33.2 11.3 %decode_attention.1.part_ref = bf16[8,16,16,640]{3,2,1,0:T(8,128)(2,1)S(1)} custom-call(s32[512]{0:T(512)S(1)} %copy-done.6, s32[64]{0:T(128)S(1)} %copy-done.7, bf16[8,16,16,576]{3,2,1,0:T(8,128)(2,1)S(1)} %get-tuple-element.7.q_ref, bf16[16,576]{1,0:T(8,128)(2,1)S(1)} %copy-done.5, bf16[64,64,576]{2,1,0:T(8,128)(2,1)} %cache_ref.1), custom_call_target="tpu_custom_call" | custom-call | tf_op jit(solution)/shard_map/decode_attention/pallas_call | solution.py:320
  44.5 0.0 copy-start
  44.5 1.5 %copy-done = bf16[8,16,16,640]{3,2,1,0:T(8,128)(2,1)} copy-done((bf16[8,16,16,640]{3,2,1,0:T(8,128)(2,1)}, bf16[8,16,16,640]{3,2,1,0:T(8,128)(2,1)S(1)}, u32[]{:S(2)}) %copy-start) | copy-done | bytes 2621464
  46.0 34.9 %prefill_attention.1 = (bf16[32,128,512]{2,1,0:T(8,128)(2,1)}, bf16[8,16,16,640]{3,2,1,0:T(8,128)(2,1)}) custom-call(s32[4]{0:T(128)} %lengths_ref.3, bf16[32,576,128]{2,1,0:T(8,128)(2,1)} %bitcast.5, bf16[8,576,128]{2,1,0:T(8,128)(2,1)} %copy-done.8, bf16[8,16,16,640]{3,2,1,0:T(8,128)(2,1)} %copy-done), custom_call_target="tpu_custom_call" | custom-call | flops 9126805504 | bytes 8912896 | tf_op jit(solution)/shard_map/prefill_attention/pallas_call | solution.py:164
  80.9 0.0 copy-done.2
  80.9 0.0 copy-start.1
  80.9 1.7 %copy-done.1 = bf16[8,16,16,640]{3,2,1,0:T(8,128)(2,1)S(1)} copy-done((bf16[8,16,16,640]{3,2,1,0:T(8,128)(2,1)S(1)}, bf16[8,16,16,640]{3,2,1,0:T(8,128)(2,1)}, u32[]{:S(2)}) %copy-start.1) | copy-done | bytes 2621464
  82.6 19.8 %output_projection.1 = bf16[16,5120]{1,0:T(8,128)(2,1)S(1)} custom-call(bf16[8,16,16,640]{3,2,1,0:T(8,128)(2,1)S(1)} %copy-done.1, bf16[16,64]{1,0:T(8,128)(2,1)S(1)} %fusion.select_ref, bf16[16,512,128]{2,1,0:T(8,128)(2,1)S(1)} %copy-done.2, bf16[2048,5120]{1,0:T(8,128)(2,1)} %weight_hbm.1), custom_call_target="tpu_custom_call" | custom-call | tf_op jit(solution)/shard_map/output_projection/pallas_call | solution.py:447
  102.4 0.0 copy-done.9
  102.4 4.4 %copy.13 = bf16[128,32,512]{2,1,0:T(8,128)(2,1)} copy(bf16[128,32,512]{2,0,1:T(8,128)(2,1)S(1)} %bitcast.4) | data formatting | bytes 8388608
  106.8 0.7 copy.15
  (4 shorter events, 0.0 us)
Async XLA Ops:
  1.4 1.0 copy-start.3
  2.4 0.9 copy-start.4
  30.1 1.0 copy-start.8
  31.1 0.7 copy-start.5
  31.8 0.7 copy-start.6
  32.5 0.7 copy-start.7
  44.5 1.5 %copy-start = (bf16[8,16,16,640]{3,2,1,0:T(8,128)(2,1)}, bf16[8,16,16,640]{3,2,1,0:T(8,128)(2,1)S(1)}, u32[]{:S(2)}) copy-start(bf16[8,16,16,640]{3,2,1,0:T(8,128)(2,1)S(1)} %decode_attention.1.part_ref) | copy-start | bytes 7864324
  46.0 34.9 %copy-start.2 = (bf16[16,512,128]{2,1,0:T(8,128)(2,1)S(1)}, bf16[16,512,128]{2,1,0:T(8,128)(2,1)}, u32[]{:S(2)}) copy-start(bf16[16,512,128]{2,1,0:T(8,128)(2,1)} %value_hbm.1) | copy-start | bytes 6291460
  80.9 1.7 %copy-start.1 = (bf16[8,16,16,640]{3,2,1,0:T(8,128)(2,1)S(1)}, bf16[8,16,16,640]{3,2,1,0:T(8,128)(2,1)}, u32[]{:S(2)}) copy-start(bf16[8,16,16,640]{3,2,1,0:T(8,128)(2,1)} %get-tuple-element.9.part_ref) | copy-start | bytes 7864324
  82.6 19.8 %copy-start.9 = (bf16[32,128,512]{2,1,0:T(8,128)(2,1)S(1)}, bf16[32,128,512]{2,1,0:T(8,128)(2,1)}, u32[]{:S(2)}) copy-start(bf16[32,128,512]{2,1,0:T(8,128)(2,1)} %get-tuple-element.8) | copy-start | bytes 12582916

commit v4 on v3

--- a/solution.py
+++ b/solution.py
@@ -22,8 +22,9 @@
 
 
 def gather_kernel(n_seq, *refs):
-    pairs = ((refs[0], refs[2]), (refs[1], refs[3]))
-    send_chip, recv_chip, send_mate, recv_mate = refs[4:]
+    send_chip, recv_chip, send_mate, recv_mate = refs[-4:]
+    count = len(refs[:-4]) // 2
+    pairs = tuple(zip(refs[:count], refs[count : 2 * count]))
     chips = n_seq // 2
     seq = lax.axis_index("seq")
     head = lax.axis_index("head")
@@ -74,11 +75,11 @@
 
 def gather(blocks, n_seq):
     vmem = pl.BlockSpec(memory_space=pltpu.VMEM)
-    dma = pltpu.SemaphoreType.DMA((2, n_seq // 2))
+    dma = pltpu.SemaphoreType.DMA((len(blocks), n_seq // 2))
     return pl.pallas_call(
         functools.partial(gather_kernel, n_seq),
-        in_specs=[vmem, vmem],
-        out_specs=[vmem, vmem],
+        in_specs=[vmem] * len(blocks),
+        out_specs=[vmem] * len(blocks),
         out_shape=[jax.ShapeDtypeStruct((n_seq, *x.shape), x.dtype) for x in blocks],
         scratch_shapes=[dma, dma, dma, dma],
         compiler_params=pltpu.CompilerParams(
@@ -88,9 +89,35 @@
     )(*blocks)
 
 
+def stat_of(level, lane):
+    high = level.astype(bf16).astype(f32)
+    middle = (level - high).astype(bf16).astype(f32)
+    low = level - high - middle
+    return jnp.where(lane == 0, high, jnp.where(lane == 1, middle, low)).astype(bf16)
+
+
+def level_of(x):
+    return (
+        x[..., LAT : LAT + 1].astype(f32)
+        + x[..., LAT + 1 : LAT + 2].astype(f32)
+        + x[..., LAT + 2 : LAT + 3].astype(f32)
+    )
+
+
+def merge(pieces):
+    levels = [level_of(x) for x in pieces]
+    top = functools.reduce(jnp.maximum, levels)
+    shares = [jnp.exp2(level - top) for level in levels]
+    total = functools.reduce(jnp.add, shares)
+    mixed = functools.reduce(
+        jnp.add, [share / total * x[..., :LAT].astype(f32) for share, x in zip(shares, pieces)]
+    )
+    return mixed, top + jnp.log2(total)
+
+
 def prefill_kernel(
     lengths_ref, q_ref, kt_ref, part_ref, out_ref, got_ref,
-    bias, keys, keys_t, queries, send_sem, recv_sem, own_sem,
+    bias, keys, keys_t, queries, from_mate, merged, send_mate, recv_mate, send_sem, recv_sem, own_sem,
 ):
     blocks, width, rows = kt_ref.shape
     total = blocks * rows
@@ -98,33 +125,50 @@
     seq = lax.axis_index("seq")
     head = lax.axis_index("head")
 
-    def exchange():
-        own = pltpu.make_async_copy(part_ref.at[seq], got_ref.at[0], own_sem)
-        return [own] + [
-            pltpu.make_async_remote_copy(
-                src_ref=part_ref.at[lax.rem(seq + d, blocks)],
-                dst_ref=got_ref.at[d],
-                send_sem=send_sem.at[d],
-                recv_sem=recv_sem.at[d],
-                device_id=(lax.rem(seq + d, blocks), head),
-                device_id_type=pl.DeviceIdType.MESH,
-            )
-            for d in range(1, blocks)
-        ]
+    chips = blocks // 2
+    chip, core = seq // 2, lax.rem(seq, 2)
+    mate = chip * 2 + 1 - core
+    order = list(range(1, chips)) + [0]
+
+    def chip_of(d):
+        return lax.rem(chip + d, chips)
+
+    def remote(source, target, send, recv, other):
+        return pltpu.make_async_remote_copy(
+            src_ref=source,
+            dst_ref=target,
+            send_sem=send,
+            recv_sem=recv,
+            device_id=(other, head),
+            device_id_type=pl.DeviceIdType.MESH,
+        )
+
+    def to_mate(d):
+        return remote(
+            part_ref.at[chip_of(d) * 2 + 1 - core],
+            from_mate.at[d],
+            send_mate.at[d],
+            recv_mate.at[d],
+            mate,
+        )
+
+    def to_chip(d):
+        if d == 0:
+            return pltpu.make_async_copy(merged.at[0], got_ref.at[0], own_sem)
+        return remote(
+            merged.at[d], got_ref.at[d], send_sem.at[d], recv_sem.at[d], chip_of(d) * 2 + core
+        )
 
     @pl.when(pl.program_id(0) == 0)
     def _():
         barrier = pltpu.get_barrier_semaphore()
-        for d in range(1, blocks):
+        for other in [mate] + [chip_of(d) * 2 + core for d in range(1, chips)]:
             pl.semaphore_signal(
-                barrier,
-                inc=1,
-                device_id=(lax.rem(seq + d, blocks), head),
-                device_id_type=pl.DeviceIdType.MESH,
+                barrier, inc=1, device_id=(other, head), device_id_type=pl.DeviceIdType.MESH
             )
-        pl.semaphore_wait(barrier, blocks - 1)
-        for copy in exchange():
-            copy.start()
+        pl.semaphore_wait(barrier, chips)
+        for d in order:
+            to_mate(d).start()
         t = lax.broadcasted_iota(jnp.int32, (rows, total), 0) + seq * rows
         k = lax.broadcasted_iota(jnp.int32, (rows, total), 1)
         bound = jnp.int32(0)
@@ -150,10 +194,21 @@
         mixed = jnp.dot(weights.astype(bf16), keys[...], preferred_element_type=f32)
         out_ref[h] = (mixed * (1.0 / sums)).astype(bf16)
 
+    @pl.when(pl.program_id(0) == 0)
+    def _():
+        shape = part_ref.shape[1:3]
+        lane = lax.broadcasted_iota(jnp.int32, (*shape, STAT), 2)
+        for d in order:
+            to_mate(d).wait()
+            both, level = merge([part_ref[chip_of(d) * 2 + core], from_mate[d]])
+            merged[d, :, :, :LAT] = both.astype(bf16)
+            merged[d, :, :, LAT:] = stat_of(level, lane)
+            to_chip(d).start()
+
     @pl.when(pl.program_id(0) == pl.num_programs(0) - 1)
     def _():
-        for copy in exchange():
-            copy.wait()
+        for d in order:
+            to_chip(d).wait()
 
 
 def prefill(prompt_lengths, queries, latents_t, part):
@@ -168,7 +223,7 @@
             pl.BlockSpec(memory_space=pltpu.SMEM),
             pl.BlockSpec((step, width, rows), lambda i: (i, 0, 0)),
             pl.BlockSpec((blocks, width, rows), lambda i: (0, 0, 0)),
-            pl.BlockSpec(memory_space=pl.ANY),
+            pl.BlockSpec(memory_space=pltpu.VMEM),
         ],
         out_specs=[
             pl.BlockSpec((step, rows, LAT), lambda i: (i, 0, 0)),
@@ -176,15 +231,16 @@
         ],
         out_shape=[
             jax.ShapeDtypeStruct((heads, rows, LAT), bf16),
-            jax.ShapeDtypeStruct(part.shape, part.dtype),
+            jax.ShapeDtypeStruct((blocks // 2, *part.shape[1:]), part.dtype),
         ],
         scratch_shapes=[
             pltpu.VMEM((rows, total), f32),
             pltpu.VMEM((total, LAT), bf16),
             pltpu.VMEM((width, total), bf16),
             pltpu.VMEM((step * rows, width), bf16),
-            pltpu.SemaphoreType.DMA((blocks,)),
-            pltpu.SemaphoreType.DMA((blocks,)),
+            pltpu.VMEM((blocks // 2, *part.shape[1:]), bf16),
+            pltpu.VMEM((blocks // 2, *part.shape[1:]), bf16),
+            *[pltpu.SemaphoreType.DMA((blocks // 2,)) for _ in range(4)],
             pltpu.SemaphoreType.DMA,
         ],
         compiler_params=pltpu.CompilerParams(
@@ -198,32 +254,6 @@
         name="prefill_attention",
     )(prompt_lengths, jnp.transpose(queries, (1, 2, 0)), latents_t, part)
     return jnp.transpose(out, (1, 0, 2)), got
-
-
-def stat_of(level, lane):
-    high = level.astype(bf16).astype(f32)
-    middle = (level - high).astype(bf16).astype(f32)
-    low = level - high - middle
-    return jnp.where(lane == 0, high, jnp.where(lane == 1, middle, low)).astype(bf16)
-
-
-def level_of(x):
-    return (
-        x[..., LAT : LAT + 1].astype(f32)
-        + x[..., LAT + 1 : LAT + 2].astype(f32)
-        + x[..., LAT + 2 : LAT + 3].astype(f32)
-    )
-
-
-def merge(pieces):
-    levels = [level_of(x) for x in pieces]
-    top = functools.reduce(jnp.maximum, levels)
-    shares = [jnp.exp2(level - top) for level in levels]
-    total = functools.reduce(jnp.add, shares)
-    mixed = functools.reduce(
-        jnp.add, [share / total * x[..., :LAT].astype(f32) for share, x in zip(shares, pieces)]
-    )
-    return mixed
 
 
 def decode_kernel(order_ref, lengths_ref, q_ref, own_ref, cache_ref, out_ref, todo, *scratch):
@@ -386,7 +416,7 @@
         copy.start()
         return copy
 
-    mixed[...] = merge([part_ref[d] for d in range(n_seq)])
+    mixed[...] = merge([part_ref[d] for d in range(part_ref.shape[0])])[0]
 
     value_copy.wait()
     for h in range(heads):
@@ -435,7 +465,8 @@
 
 
 def tail(part, select, value_up, out_weight, n_head):
-    n_seq, rows, heads, wide = part.shape
+    _, rows, heads, wide = part.shape
+    n_seq = lax.axis_size("seq")
     depth, width = out_weight.shape
     owners = n_seq
     while width // owners % 128:
@@ -487,7 +518,8 @@
 ):
     n_head = lax.axis_size("head")
     rows = dec_queries.shape[0]
-    queries, latents_t = gather((dec_queries, prefill_latents.T), lax.axis_size("seq"))
+    latents_t = lax.all_gather(prefill_latents.T, "seq", axis=0)
+    (queries,) = gather((dec_queries,), lax.axis_size("seq"))
     part = decode(page_order, dec_lengths, queries, dec_new_latent, cache_pages)
     prefill_out, part = prefill(prompt_lengths, prefill_queries, latents_t, part)
     members = lax.dynamic_slice_in_dim(group_members, lax.axis_index("head") * rows, rows)

time: 108 us -> 110 us (1.019); the launches traced: 107 us -> 108 us
  between operations: 0.71 us -> 14.1 us
  Pallas kernels: 92.7 us -> 81.8 us
  local copies, waits for them, and re-layouts: 14 us -> 11.6 us
    pallas_call x1, Pallas kernels: 34.9 us -> 27.8 us  [prefill(): pl.pallas_call(prefill_kernel, grid=(heads // step,), in_specs=[pl.BlockS...]
    pallas_call x1, Pallas kernels: 26.7 us -> 22.4 us  [gather(): pl.pallas_call(functools.partial(gather_kernel, n_seq), in_specs=[vmem] *...]
    unnamed x22 -> x18, local copies, waits for them, and re-layouts: 13.2 us -> 10.9 us
  transfers between devices with their start and end apart: 0 -> 1, of which waited for: 0 -> 0; matrix products, arithmetic and copies ran while one was open for 0% -> 1% of each run, Pallas kernels for 0% -> 31%
where the time goes in v4:
time: 110 us; the launch traced here: 108 us
  Pallas kernels  81.8 us (74%)
  between operations  14.1 us (13%)
  local copies, waits for them, and re-layouts  11.6 us (11%)
    pallas_call x1, Pallas kernels, prefill(): pl.pallas_call(prefill_kernel, grid=(heads // step,), in_specs=[pl.BlockS...  27.8 us
    pallas_call x1, Pallas kernels, gather(): pl.pallas_call(functools.partial(gather_kernel, n_seq), in_specs=[vmem] *...  22.4 us
    pallas_call x1, Pallas kernels, tail(): pl.pallas_call(functools.partial(tail_kernel, n_seq, n_head), in_specs=[v...  20.3 us
    pallas_call x1, Pallas kernels, decode(): pl.pallas_call(decode_kernel, in_specs=[smem, smem, vmem, vmem, vmem], ou...  11.3 us
    unnamed x18, local copies, waits for them, and re-layouts  10.9 us
  transfers between devices with their start and end apart: 1, of which 0 were waited for; matrix products, arithmetic and copies ran while one was open for 1% of the time, Pallas kernels for 31%

profile of v4, /device:TPU:0, one launch (start us, length us, event | category | flops | bytes accessed | tf_op | source)
XLA Modules:
  0.0 108.3 jit_solution(16967733787651415416)
XLA Ops:
  7.2 0.0 all-gather.3.cloned.1.call-start
  7.2 0.7 all-gather.3.cloned.1.call-update
  7.9 0.0 copy-start.3
  7.9 1.0 copy-done.3
  8.9 22.4 %gather_over_seq.1.q_ref = bf16[8,16,16,576]{3,2,1,0:T(8,128)(2,1)S(1)} custom-call(bf16[16,16,576]{2,1,0:T(8,128)(2,1)S(1)} %copy-done.3), custom_call_target="tpu_custom_call" | custom-call | tf_op jit(solution)/shard_map/gather_over_seq/pallas_call | solution.py:79
  31.2 0.7 dynamic_slice.3
  32.0 0.0 copy-start.4
  32.0 0.7 copy-done.4
  32.7 0.0 copy-start.5
  32.7 0.7 copy-done.5
  33.4 0.0 copy-start.6
  33.4 0.7 copy-done.6
  34.0 11.3 %decode_attention.1.part_ref = bf16[8,16,16,640]{3,2,1,0:T(8,128)(2,1)S(1)} custom-call(s32[512]{0:T(512)S(1)} %copy-done.5, s32[64]{0:T(128)S(1)} %copy-done.6, bf16[8,16,16,576]{3,2,1,0:T(8,128)(2,1)S(1)} %gather_over_seq.1.q_ref, bf16[16,576]{1,0:T(8,128)(2,1)S(1)} %copy-done.4, bf16[64,64,576]{2,1,0:T(8,128)(2,1)} %cache_ref.1), custom_call_target="tpu_custom_call" | custom-call | tf_op jit(solution)/shard_map/decode_attention/pallas_call | solution.py:350
  45.4 0.0 copy-start
  45.4 1.5 %copy-done = bf16[8,16,16,640]{3,2,1,0:T(8,128)(2,1)} copy-done((bf16[8,16,16,640]{3,2,1,0:T(8,128)(2,1)}, bf16[8,16,16,640]{3,2,1,0:T(8,128)(2,1)S(1)}, u32[]{:S(2)}) %copy-start) | copy-done | bytes 2621464
  46.9 0.1 fusion.select_ref
  47.0 27.8 %prefill_attention.1 = (bf16[32,128,512]{2,1,0:T(8,128)(2,1)}, bf16[4,16,16,640]{3,2,1,0:T(8,128)(2,1)}) custom-call(s32[4]{0:T(128)} %lengths_ref.3, bf16[32,576,128]{2,1,0:T(8,128)(2,1)} %bitcast.6, bf16[8,576,128]{2,1,0:T(8,128)(2,1)} %bitcast.7, bf16[8,16,16,640]{3,2,1,0:T(8,128)(2,1)} %copy-done), custom_call_target="tpu_custom_call" | custom-call | flops 9126805504 | bytes 8912896 | tf_op jit(solution)/shard_map/prefill_attention/pallas_call | solution.py:219
  74.8 0.0 copy-done.1
  74.8 0.0 copy-start.2
  74.8 1.3 %copy-done.2 = bf16[4,16,16,640]{3,2,1,0:T(8,128)(2,1)S(1)} copy-done((bf16[4,16,16,640]{3,2,1,0:T(8,128)(2,1)S(1)}, bf16[4,16,16,640]{3,2,1,0:T(8,128)(2,1)}, u32[]{:S(2)}) %copy-start.2) | copy-done | bytes 1310744
  76.1 20.3 %output_projection.1 = bf16[16,5120]{1,0:T(8,128)(2,1)S(1)} custom-call(bf16[4,16,16,640]{3,2,1,0:T(8,128)(2,1)S(1)} %copy-done.2, bf16[16,64]{1,0:T(8,128)(2,1)S(1)} %fusion.select_ref, bf16[16,512,128]{2,1,0:T(8,128)(2,1)S(1)} %copy-done.1, bf16[2048,5120]{1,0:T(8,128)(2,1)} %weight_hbm.1), custom_call_target="tpu_custom_call" | custom-call | tf_op jit(solution)/shard_map/output_projection/pallas_call | solution.py:478
  96.4 0.0 copy-done.7
  96.4 4.4 %copy.13 = bf16[128,32,512]{2,1,0:T(8,128)(2,1)} copy(bf16[128,32,512]{2,0,1:T(8,128)(2,1)S(1)} %bitcast.4) | data formatting | bytes 8388608
  100.8 0.7 copy.15
  (3 shorter events, 0.0 us)
Async XLA Ops:
  7.2 39.8 %all-gather.3.cloned.1.call-start = ((), (), s32[]{:S(2)}) async-start(), calls=%async_computation | async-start | bytes 1327104 | tf_op jit(solution)/shard_map/all_gather | solution.py:521
  7.9 1.0 copy-start.3
  32.0 0.7 copy-start.4
  32.7 0.7 copy-start.5
  33.4 0.7 copy-start.6
  45.4 1.5 %copy-start = (bf16[8,16,16,640]{3,2,1,0:T(8,128)(2,1)}, bf16[8,16,16,640]{3,2,1,0:T(8,128)(2,1)S(1)}, u32[]{:S(2)}) copy-start(bf16[8,16,16,640]{3,2,1,0:T(8,128)(2,1)S(1)} %decode_attention.1.part_ref) | copy-start | bytes 7864324
  47.0 27.8 %copy-start.1 = (bf16[16,512,128]{2,1,0:T(8,128)(2,1)S(1)}, bf16[16,512,128]{2,1,0:T(8,128)(2,1)}, u32[]{:S(2)}) copy-start(bf16[16,512,128]{2,1,0:T(8,128)(2,1)} %value_hbm.1) | copy-start | bytes 6291460
  74.8 1.3 %copy-start.2 = (bf16[4,16,16,640]{3,2,1,0:T(8,128)(2,1)S(1)}, bf16[4,16,16,640]{3,2,1,0:T(8,128)(2,1)}, u32[]{:S(2)}) copy-start(bf16[4,16,16,640]{3,2,1,0:T(8,128)(2,1)} %get-tuple-element.5.part_ref) | copy-start | bytes 3932164
  76.1 20.3 %copy-start.7 = (bf16[32,128,512]{2,1,0:T(8,128)(2,1)S(1)}, bf16[32,128,512]{2,1,0:T(8,128)(2,1)}, u32[]{:S(2)}) copy-start(bf16[32,128,512]{2,1,0:T(8,128)(2,1)} %get-tuple-element.4) | copy-start | bytes 12582916
Sparse Core Ops, SparseCore 0:
  9.9 28.3 all-gather.2
